TPU v7x, 32 devices: a whole 2x2x4 slice. The times are simulated.
32 devices in a mesh: lyr: 2 (over core), strip: 16 (over z, y, x).
Axes of the slice: x: 2, y: 2, z: 4, core: 2. Of those that a mesh axis runs over, the one named last changes fastest.
Arguments:
- nodes: bfloat16 [2, 2, 64, 128, 128], P('lyr', None, None, 'strip'), may hold values from -6 to 6
- upstream: bfloat16 [2, 2, 64, 128, 128], P('lyr', None, None, 'strip'), may hold values from -6 to 6
- usage: int32 [2, 2, 128, 128], P('lyr', None, 'strip'), may hold values from 0 to 15
- blockage: int32 [2, 2, 2, 128, 128], P('lyr', None, None, 'strip'), may hold values 0 or 1
- capacity: int32 [2, 2, 2, 128, 128], P('lyr', None, None, 'strip'), may hold values from 1 to 8
- w_src: bfloat16 [2, 128, 64], replicated, may hold values from -0.75 to 0.75
- w_dst: bfloat16 [2, 128, 64], replicated, may hold values from -0.75 to 0.75
- w_out: bfloat16 [2, 64, 128], replicated, may hold values from -0.5 to 0.5
Outputs:
- grad_nodes: bfloat16 [2, 2, 64, 128, 128], P('lyr', None, None, 'strip')
- grad_src: float32 [2, 128, 64], replicated
- grad_dst: float32 [2, 128, 64], replicated
- grad_out: float32 [2, 64, 128], replicated
All inputs are finite; a program needn't handle non-finite values. No bound on the sum of `blockage` on one device may be relied on, other than what follows from the above.
Results may differ from a plain program's by a relative error of at most 0.0058.
Values may be sent and summed in bfloat16 or wider, within the bound.
A program may use at most 128 MiB of HBM per device.

v0:
```python
import math

import jax
import jax.numpy as jnp
from jax import lax
from jax.sharding import PartitionSpec as P


def from_behind(value, axis, steps):
    count = lax.axis_size(axis)
    initial, last = (max(0, -steps), min(count, count - steps))
    return lax.ppermute(value, axis, [(source, source + steps) for source in range(initial, last)])


def edge_grads(w_src, w_dst, w_out, x_u, x_v, d_u, d_v, gate):
    feat, rows, cols = x_u.shape
    count = rows * cols
    flat_u = x_u.reshape(feat, count)
    flat_v = x_v.reshape(feat, count)
    pre = jnp.dot(w_src, flat_u, preferred_element_type=jnp.float32) + jnp.dot(
        w_dst, flat_v, preferred_element_type=jnp.float32
    )
    sigma = jax.nn.sigmoid(pre)
    act = (pre * sigma).astype(jnp.bfloat16)
    slope = sigma * (1.0 + pre * (1.0 - sigma))
    diff = d_v.astype(jnp.float32) - d_u.astype(jnp.float32)
    g_msg = (gate[None] * diff).reshape(feat, count).astype(jnp.bfloat16)
    g_act = lax.dot_general(
        w_out, g_msg, (((0,), (0,)), ((), ())), preferred_element_type=jnp.float32
    )
    g_pre = (g_act * slope).astype(jnp.bfloat16)
    g_out = lax.dot_general(
        g_msg, act, (((1,), (1,)), ((), ())), preferred_element_type=jnp.float32
    )
    g_src = lax.dot_general(
        g_pre, flat_u, (((1,), (1,)), ((), ())), preferred_element_type=jnp.float32
    )
    g_dst = lax.dot_general(
        g_pre, flat_v, (((1,), (1,)), ((), ())), preferred_element_type=jnp.float32
    )
    gx_u = lax.dot_general(
        w_src, g_pre, (((0,), (0,)), ((), ())), preferred_element_type=jnp.float32
    )
    gx_v = lax.dot_general(
        w_dst, g_pre, (((0,), (0,)), ((), ())), preferred_element_type=jnp.float32
    )
    return (gx_u.reshape(feat, rows, cols), gx_v.reshape(feat, rows, cols), (g_src, g_dst, g_out))


def on_device(nodes, upstream, usage, blockage, capacity, w_src, w_dst, w_out):
    pair = lax.axis_index("lyr")
    strip_at = lax.axis_index("strip")
    n_pairs = lax.axis_size("lyr")
    feat = nodes.shape[2]
    rows = nodes.shape[3]
    cols = nodes.shape[4]
    damp = lax.rsqrt(1.0 + usage[0].astype(jnp.float32))[:, None]
    feats = (nodes[0].astype(jnp.float32) * damp).astype(jnp.bfloat16)
    grads_in = upstream[0]
    gates = (1 - blockage[0]).astype(jnp.float32) * capacity[0].astype(jnp.float32) * 0.25
    row_first = pair % 2 == 0
    x_row = jnp.where(row_first, feats[0], feats[1])
    d_row = jnp.where(row_first, grads_in[0], grads_in[1])
    gate_row = jnp.where(row_first, gates[0, 0], gates[1, 0])
    x_col = jnp.where(row_first, feats[1], feats[0])
    d_col = jnp.where(row_first, grads_in[1], grads_in[0])
    gate_col = jnp.where(row_first, gates[1, 0], gates[0, 0])
    rim = from_behind(jnp.stack((x_row[:, 0, :], d_row[:, 0, :])), "strip", -1)
    x_next = jnp.concatenate((x_row[:, 1:, :], rim[0][:, None, :]), 1)
    d_next = jnp.concatenate((d_row[:, 1:, :], rim[1][:, None, :]), 1)
    row_ids = strip_at * rows + jnp.arange(rows)
    gate_r = gate_row * (row_ids < cols - 1).astype(jnp.float32)[:, None]
    gu_r, gv_r, w_rowwise = edge_grads(
        w_src[0], w_dst[0], w_out[0], x_row, x_next, d_row, d_next, gate_r
    )
    back = from_behind(gv_r[:, -1, :].astype(jnp.bfloat16), "strip", 1).astype(jnp.float32)
    add_row = gu_r + jnp.concatenate((back[:, None, :], gv_r[:, :-1, :]), 1)
    x_side = jnp.concatenate((x_col[:, :, 1:], jnp.zeros((feat, rows, 1), jnp.bfloat16)), 2)
    d_side = jnp.concatenate((d_col[:, :, 1:], jnp.zeros((feat, rows, 1), jnp.bfloat16)), 2)
    gate_c = gate_col * (jnp.arange(cols) < cols - 1).astype(jnp.float32)[None, :]
    gu_c, gv_c, w_colwise = edge_grads(
        w_src[0], w_dst[0], w_out[0], x_col, x_side, d_col, d_side, gate_c
    )
    add_col = gu_c + jnp.concatenate((jnp.zeros((feat, rows, 1), jnp.float32), gv_c[:, :, :-1]), 2)
    planar = tuple((a + b for a, b in zip(w_rowwise, w_colwise)))
    gu_0, gv_0, w_inner = edge_grads(
        w_src[1], w_dst[1], w_out[1], feats[0], feats[1], grads_in[0], grads_in[1], gates[0, 1]
    )
    packed = jnp.stack((feats[0], grads_in[0]))
    turned = lax.all_to_all(packed, "strip", split_axis=3, concat_axis=2, tiled=True)
    above = jnp.swapaxes(from_behind(turned, "lyr", -1), 2, 3)
    gate_x = gates[1, 1] * (pair < n_pairs - 1).astype(jnp.float32)
    gu_x, gv_x, w_cross = edge_grads(
        w_src[1], w_dst[1], w_out[1], feats[1], above[0], grads_in[1], above[1], gate_x
    )
    flipped = jnp.swapaxes(gv_x, 1, 2)
    spread = lax.all_to_all(
        flipped.astype(jnp.bfloat16), "strip", split_axis=1, concat_axis=2, tiled=True
    ).astype(flipped.dtype)
    returned = from_behind(spread.astype(jnp.bfloat16), "lyr", 1).astype(spread.dtype)
    layer_low = jnp.where(row_first, add_row, add_col) + gu_0 + returned
    layer_high = jnp.where(row_first, add_col, add_row) + gv_0 + gu_x
    node_sum = jnp.stack((layer_low, layer_high))
    grad_nodes = (grads_in.astype(jnp.float32) + damp * node_sum).astype(jnp.bfloat16)[None]
    vias = tuple((a + b for a, b in zip(w_inner, w_cross)))
    joined = (
        jnp.stack((planar[0], vias[0])),
        jnp.stack((planar[1], vias[1])),
        jnp.stack((planar[2], vias[2])),
    )
    joined = lax.psum((joined[0], joined[1], joined[2]), ("lyr", "strip"))
    scale = 1.0 / math.sqrt(2 * n_pairs * cols * cols)
    return (grad_nodes, joined[0] * scale, joined[1] * scale, joined[2] * scale)


def solution(mesh):
    placed = (
        P("lyr", None, None, "strip", None),
        P("lyr", None, None, "strip", None),
        P("lyr", None, "strip", None),
        P("lyr", None, None, "strip", None),
        P("lyr", None, None, "strip", None),
        P(),
        P(),
        P(),
    )
    return jax.shard_map(
        on_device,
        mesh=mesh,
        in_specs=placed,
        out_specs=(P("lyr", None, None, "strip", None), P(), P(), P()),
        check_vma=False,
    )
```

profile of v0, /device:TPU:0, one launch (start us, length us, event | category | flops | bytes accessed | tf_op | source)
XLA Modules:
  0.0 218.1 jit_solution(791288954664966132)
XLA Ops:
  7.2 1.0 fusion.145
  8.3 0.6 copy-done.48
  9.0 0.9 fusion.96
  10.0 0.7 pad_maximum_fusion.5
  10.6 1.3 collective-permute-start
  12.4 1.1 reshape.305
  13.5 10.1 %all-to-all-start = ((bf16[16,2,4096]{2,1,0:T(2,128)(2,1)}), bf16[16,2,4096]{2,1,0:T(2,128)(2,1)}, u32[]{:S(2)}, u32[]{:S(2)}) async-start(bf16[16,2,4096]{2,1,0:T(2,128)(2,1)} %reshape.305), calls=%async_computation | async-start | bytes 524288 | tf_op jit(solution)/shard_map/all_to_all | solution.py:90
  23.7 0.7 copy.83
  24.6 0.7 copy-done.29
  26.3 0.6 fusion.139
  27.1 0.7 copy-done.15
  28.8 0.8 fusion.44
  29.6 0.8 fusion.50
  31.8 0.8 bitcast_multiply_fusion.2
  33.8 0.9 convolution_bitcast_fusion.5
  35.0 0.7 copy-done.14
  35.9 0.8 copy-done.13
  36.9 0.6 copy-done.59
  37.5 0.9 fusion.33
  38.5 0.6 bitcast_multiply_fusion
  39.1 0.7 slice.142
  39.7 0.7 slice.136
  40.4 1.0 copy.78
  41.4 0.9 copy.109
  42.9 1.1 copy.119
  44.1 0.7 slice_bitcast_fusion.1
  44.9 1.2 fusion.6
  46.4 0.7 copy-done.19
  47.2 0.9 fusion.18
  48.5 0.6 copy-done.4
  49.2 0.8 fusion.16
  50.4 4.5 %collective-permute-start.1 = (bf16[64,128]{1,0:T(8,128)(2,1)S(1)}, bf16[64,128]{1,0:T(8,128)(2,1)}, u32[]{:S(2)}, u32[]{:S(2)}) collective-permute-start(bf16[64,128]{1,0:T(8,128)(2,1)S(1)} %bitcast.381), channel_id=1, source_target_pairs={{0,1},{1,2},{2,3},{3,4},{4,5},{5,6},{6,7},{7,8},{8,9},{9,10},{10,1... | collective-permute-start | bytes 49160 | tf_op jit(solution)/shard_map/ppermute | solution.py:12
  54.9 0.8 fusion.68
  55.7 0.9 convolution_bitcast_fusion.10
  56.6 1.3 reshape.306
  57.9 0.9 copy.100
  58.9 2.0 copy.101
  60.9 1.4 collective-permute-start.2
  62.4 0.8 fusion.14
  63.2 1.0 copy.123
  64.4 0.7 bitcast_convert_fusion
  65.1 0.7 copy.87
  65.8 1.0 slice_convert_fusion
  67.0 0.8 copy-done.2
  67.7 1.0 fusion.31
  68.8 0.7 copy-done.17
  70.8 0.5 copy-done.32
  71.5 0.9 copy.112
  72.4 0.8 fusion.13
  73.2 0.8 fusion.15
  74.2 0.7 copy-done.37
  75.0 1.4 fusion.17
  76.4 0.6 pad_maximum_fusion.4
  77.2 0.6 pad_maximum_fusion.3
  78.0 0.6 pad_maximum_fusion.2
  78.6 0.9 reshape.307
  79.5 5.0 %all-to-all-start.1 = ((bf16[16,2,2048]{2,1,0:T(2,128)(2,1)}), bf16[16,2,2048]{2,1,0:T(2,128)(2,1)S(1)}, u32[]{:S(2)}, u32[]{:S(2)}) async-start(bf16[16,2,2048]{2,1,0:T(2,128)(2,1)} %reshape.307), calls=%async_computation.1 | async-start | bytes 262144 | tf_op jit(solution)/shard_map/all_to_all | solution.py:97
  84.7 119.2 %all-reduce.6.cloned.1.call-done = (f32[2,128,64]{1,2,0:T(8,128)}, f32[2,128,64]{1,2,0:T(8,128)}, f32[2,64,128]{2,1,0:T(8,128)}) async-done(((f32[2,128,64]{1,2,0:T(8,128)}, f32[2,128,64]{1,2,0:T(8,128)}, f32[2,64,128]{2,1,0:T(8,128)}), (f32[2,128,64]{1,2,0:T(8,128)}, f32[2,128,64]{1,2,0:T(8,128)}, f32[2,64,128]{2,1,0:T(8,128)})) %all-reduce.6.cloned.1.call-update) | async-done | bytes 196624 | tf_op jit(solution)/shard_map/psum | solution.py:111
  203.9 1.5 broadcast_multiply_fusion
  205.4 0.6 broadcast_multiply_fusion.1
  206.3 1.4 collective-permute-start.3
  207.8 0.6 broadcast_multiply_fusion.2
  209.3 0.7 copy-done
  210.3 0.9 copy.113
  (186 shorter events, 12.1 us)
Async XLA Ops:
  7.2 1.1 copy-start.57
  7.2 1.7 copy-start.35
  8.2 18.7 %copy-start.1 = (bf16[1,1,64,8,128]{4,3,2,1,0:T(8,128)(2,1)}, bf16[1,1,64,8,128]{4,3,2,1,0:T(8,128)(2,1)S(1)}, u32[]{:S(2)}) copy-start(bf16[1,1,64,8,128]{4,3,2,1,0:T(8,128)(2,1)S(1)} %get-tuple-element.30) | copy-start | bytes 393220
  10.0 2.0 copy-start.24
  10.0 22.6 %copy-start.27 = (bf16[64,8,128]{2,0,1:T(8,128)(2,1)}, bf16[64,8,128]{2,0,1:T(8,128)(2,1)S(1)}, u32[]{:S(2)}) copy-start(bf16[64,8,128]{2,0,1:T(8,128)(2,1)S(1)} %get-tuple-element.22) | copy-start | bytes 393220
  10.6 33.5 %collective-permute-start = (bf16[2,64,128]{2,1,0:T(8,128)(2,1)}, bf16[2,64,128]{2,1,0:T(8,128)(2,1)}, u32[]{:S(2)}, u32[]{:S(2)}) collective-permute-start(bf16[2,64,128]{2,1,0:T(8,128)(2,1)} %pad_maximum_fusion.5), channel_id=1, source_target_pairs={{1,0},{2,1},{3,2},{4,3},{5,4},{6,5},{7,6},{8,7},{9,8},{10,9},{11,1... | collective-permute-start | bytes 98312 | tf_op jit(solution)/shard_map/ppermute | solution.py:12
  13.5 43.1 %all-to-all-start = ((bf16[16,2,4096]{2,1,0:T(2,128)(2,1)}), bf16[16,2,4096]{2,1,0:T(2,128)(2,1)}, u32[]{:S(2)}, u32[]{:S(2)}) async-start(bf16[16,2,4096]{2,1,0:T(2,128)(2,1)} %reshape.305), calls=%async_computation | async-start | bytes 524288 | tf_op jit(solution)/shard_map/all_to_all | solution.py:90
  23.6 180.3 %all-reduce.6.cloned.1.call-start = ((), (), s32[]{:S(2)}) async-start(), calls=%async_computation.2 | async-start | bytes 393216 | tf_op jit(solution)/shard_map/psum | solution.py:111
  24.5 5.1 %copy-start.3 = (bf16[1,64,8,128]{3,2,1,0:T(8,128)(2,1)}, bf16[1,64,8,128]{3,2,1,0:T(8,128)(2,1)S(1)}, u32[]{:S(2)}) copy-start(bf16[1,64,8,128]{3,2,1,0:T(8,128)(2,1)S(1)} %copy.95) | copy-start | bytes 393220
  24.5 0.8 copy-start.29
  27.0 0.8 copy-start.15
  28.0 0.8 copy-start.20
  31.1 1.5 copy-start.44
  31.8 1.1 copy-start.18
  33.8 0.9 copy-start.23
  33.8 0.9 copy-start.30
  34.7 1.0 copy-start.14
  35.7 0.9 copy-start.13
  35.7 1.2 copy-start.21
  35.8 1.0 copy-start.36
  37.5 2.2 %copy-start.25 = (bf16[64,8,128]{2,0,1:T(8,128)(2,1)S(1)}, bf16[64,8,128]{2,0,1:T(8,128)(2,1)}, u32[]{:S(2)}) copy-start(bf16[64,8,128]{2,0,1:T(8,128)(2,1)} %copy-done.24) | copy-start | bytes 393220
  38.4 2.0 copy-start.10
  40.4 1.0 copy-start.12
  44.1 0.8 copy-start.16
  44.8 1.2 copy-start.38
  44.8 1.2 copy-start.47
  44.8 1.2 copy-start.63
  46.1 1.0 copy-start.19
  46.1 1.1 copy-start.28
  46.1 1.1 copy-start.45
  46.1 1.1 copy-start.62
  47.2 0.9 copy-start.26
  47.2 0.9 copy-start.60
  47.2 0.9 copy-start.65
  48.1 0.9 copy-start.4
  50.3 5.4 %copy-start.6 = (f32[8,8,8,128]{3,2,1,0:T(8,128)}, f32[8,8,8,128]{3,2,1,0:T(8,128)S(1)}, u32[]{:S(2)}) copy-start(f32[8,8,8,128]{3,2,1,0:T(8,128)S(1)} %copy.132) | copy-start | bytes 786436
  50.3 4.6 %copy-start.33 = (bf16[64,7,128]{2,0,1:T(8,128)(2,1)S(1)}, bf16[64,7,128]{2,0,1:T(8,128)(2,1)}, u32[]{:S(2)}) copy-start(bf16[64,7,128]{2,0,1:T(8,128)(2,1)} %slice.142) | copy-start | bytes 344068
  50.4 5.3 %copy-start.31 = (bf16[2,128,64]{1,2,0:T(8,128)(2,1)S(1)}, bf16[2,128,64]{1,2,0:T(8,128)(2,1)}, u32[]{:S(2)}) copy-start(bf16[2,128,64]{1,2,0:T(8,128)(2,1)} %param.13) | copy-start | bytes 98308
  50.4 14.0 %collective-permute-start.1 = (bf16[64,128]{1,0:T(8,128)(2,1)S(1)}, bf16[64,128]{1,0:T(8,128)(2,1)}, u32[]{:S(2)}, u32[]{:S(2)}) collective-permute-start(bf16[64,128]{1,0:T(8,128)(2,1)S(1)} %bitcast.381), channel_id=1, source_target_pairs={{0,1},{1,2},{2,3},{3,4},{4,5},{5,6},{6,7},{7,8},{8,9},{9,10},{10,1... | collective-permute-start | bytes 49160 | tf_op jit(solution)/shard_map/ppermute | solution.py:12
  58.9 3.5 %copy-start.9 = (bf16[64,8,128]{2,1,0:T(8,128)(2,1)S(1)}, bf16[64,8,128]{2,1,0:T(8,128)(2,1)}, u32[]{:S(2)}) copy-start(bf16[64,8,128]{2,1,0:T(8,128)(2,1)} %copy-done.8) | copy-start | bytes 393220
  58.9 3.5 %copy-start.52 = (f32[128,64]{0,1:T(8,128)S(1)}, f32[128,64]{0,1:T(8,128)}, u32[]{:S(2)}) copy-start(f32[128,64]{0,1:T(8,128)} %fusion.68) | copy-start | bytes 98308
  60.9 2.2 %copy-start.7 = (f32[8,8,8,128]{3,2,1,0:T(8,128)S(1)}, f32[8,8,8,128]{3,2,1,0:T(8,128)}, u32[]{:S(2)}) copy-start(f32[8,8,8,128]{3,2,1,0:T(8,128)} %copy-done.6) | copy-start | bytes 786436
  60.9 4.9 %collective-permute-start.2 = (bf16[2,64,128,8]{2,1,3,0:T(8,128)(2,1)}, bf16[2,64,128,8]{2,1,3,0:T(8,128)(2,1)}, u32[]{:S(2)}, u32[]{:S(2)}) collective-permute-start(bf16[2,64,128,8]{2,1,3,0:T(8,128)(2,1)} %copy.101), channel_id=1, source_target_pairs={{16,0},{17,1},{18,2},{19,3},{20,4},{21,5},{22,6},{23,7},{24,8},{25... | collective-permute-start | bytes 786440 | tf_op jit(solution)/shard_map/ppermute | solution.py:12
  63.2 1.0 copy-start.11
  65.8 1.1 copy-start.54
  66.8 0.9 copy-start.2
  68.7 0.8 copy-start.17
  69.7 1.0 copy-start.22
  70.5 0.8 copy-start.32
  71.5 0.9 copy-start.43
  72.4 0.8 copy-start.42
  74.0 1.0 copy-start.37
  74.0 0.9 copy-start.58
  75.0 1.4 copy-start.53
  76.4 0.8 copy-start.40
  77.2 0.8 copy-start.46
  79.5 126.5 %all-to-all-start.1 = ((bf16[16,2,2048]{2,1,0:T(2,128)(2,1)}), bf16[16,2,2048]{2,1,0:T(2,128)(2,1)S(1)}, u32[]{:S(2)}, u32[]{:S(2)}) async-start(bf16[16,2,2048]{2,1,0:T(2,128)(2,1)} %reshape.307), calls=%async_computation.1 | async-start | bytes 262144 | tf_op jit(solution)/shard_map/all_to_all | solution.py:97
  203.9 1.5 copy-start.51
  206.3 2.7 %copy-start.5 = (f32[64,7,128]{0,2,1:T(8,128)S(1)}, f32[64,7,128]{0,2,1:T(8,128)}, u32[]{:S(2)}) copy-start(f32[64,7,128]{0,2,1:T(8,128)} %copy.123) | copy-start | bytes 688132
  206.3 1.5 copy-start.50
  206.3 2.6 %collective-permute-start.3 = (bf16[64,8,128]{0,2,1:T(8,128)(2,1)S(1)}, bf16[64,8,128]{0,2,1:T(8,128)(2,1)S(1)}, u32[]{:S(2)}, u32[]{:S(2)}) collective-permute-start(bf16[64,8,128]{0,2,1:T(8,128)(2,1)S(1)} %bitcast.377), channel_id=1, source_target_pairs={{0,16},{1,17},{2,18},{3,19},{4,20},{5,21},{6,22},{7,23},{8,24},{9,... | collective-permute-start | bytes 393224 | tf_op jit(solution)/shard_map/ppermute | solution.py:12
  207.8 1.1 copy-start.34
  208.9 1.0 copy-start
  208.9 1.0 copy-start.49
  (10 other events, 7.1 us)
Sparse Core Ops, SparseCore 0:
  78.7 125.1 all-reduce.5
where the time goes:
time: 221 us; the launch traced here: 218 us
  waiting for transfers between devices  120 us (54%)
  local copies, waits for them, and re-layouts  31.4 us (14%)
  starting transfers between devices  23.7 us (11%)
  matrix products  16.6 us (8%)
  between operations  14.9 us (7%)
  other arithmetic  11.7 us (5%)
    psum x1, waiting for transfers between devices, on_device(): joined = lax.psum((joined[0], joined[1], joined[2]), ('lyr', 'strip'))  119 us
    unnamed x146, local copies, waits for them, and re-layouts  18.1 us
    all_to_all x1, starting transfers between devices, on_device(): lax.all_to_all(packed, 'strip', split_axis=3, concat_axis=2, tiled=True)  10.1 us
    ppermute x4, starting transfers between devices, from_behind(): lax.ppermute(value, axis, [(source, source + steps) for source in range(i...  8.63 us
    all_to_all x1, starting transfers between devices, on_device(): lax.all_to_all(flipped.astype(jnp.bfloat16), 'strip', split_axis=1, conca...  4.97 us
  transfers between devices with their start and end apart: 7, of which 2 were waited for; matrix products, arithmetic and copies ran while one was open for 16% of the time, Pallas kernels for 0%

commit v1 on v0

v1 whole, which is shorter than its diff:
```python
import functools
import math

import jax
import jax.numpy as jnp
from jax import lax
from jax.experimental import pallas as pl
from jax.experimental.pallas import tpu as pltpu
from jax.sharding import PartitionSpec as P

MESH = pl.DeviceIdType.MESH
F32 = jnp.float32
BF16 = jnp.bfloat16
TILE = 16


def mm(a, b):
    return jnp.dot(a, b, preferred_element_type=F32)


def edges(xu, xv, gate, w):
    both = jnp.concatenate((xu, xv), 1)
    y = mm(both, w)
    half = w.shape[1] // 2
    pre, raw = y[:, :half], y[:, half:]
    s = 0.5 * jnp.tanh(0.5 * pre) + 0.5
    act = pre * s
    slope = s + act * (1.0 - s)
    gate = gate.astype(F32)
    return both, (gate * raw * slope).astype(BF16), (gate * act).astype(BF16)


def weight_sums(gp, ga, both):
    left = jnp.concatenate((gp, ga), 1)
    return lax.dot_general(left, both, (((0,), (0,)), ((), ())), preferred_element_type=F32)


def kernel(
    pairs, strips, rows, cols, chunk,
    xd, s_up, s_dn, gb, w1, pw, vw,
    acc, w_sum,
    prev_x, next_x, prev_g, below, above, gps, wacc, wpart, wrecv, wres,
    halo_send, halo_recv, cross_send, cross_recv, red_send, red_recv,
):
    p = lax.axis_index("lyr")
    s = lax.axis_index("strip")
    devices = pairs * strips
    flat = p * strips + s
    owners = wpart.shape[0]
    cells = rows * cols
    step = chunk * cols
    square = rows * rows

    def place(k):
        target = lax.rem(flat + k, devices)
        return target, (lax.div(target, strips), lax.rem(target, strips))

    barrier = pltpu.get_barrier_semaphore()

    @pl.loop(1, devices)
    def _(k):
        pl.semaphore_signal(barrier, inc=1, device_id=place(k)[1], device_id_type=MESH)

    pl.semaphore_wait(barrier, devices - 1)

    jr = lax.rem(p, 2)
    jc = 1 - jr

    def send(src, dst, a, b, to):
        copy = pltpu.make_async_remote_copy(
            src_ref=src, dst_ref=dst, send_sem=a, recv_sem=b, device_id=to, device_id_type=MESH
        )
        copy.start()
        return copy

    def wait_bytes(ref, sem):
        pltpu.make_async_copy(ref, ref, sem).wait()

    @pl.loop(0, strips)
    def _(k):
        t = lax.rem(s + k, strips)

        @pl.when(p < pairs - 1)
        def _():
            send(s_up.at[t], below.at[s], cross_send.at[0], cross_recv.at[0], (p + 1, t))

        @pl.when(p > 0)
        def _():
            send(s_dn.at[t], above.at[s], cross_send.at[1], cross_recv.at[1], (p - 1, t))

    after = (p, lax.rem(s + 1, strips))
    before = (p, lax.rem(s + strips - 1, strips))
    last = pl.ds(cells - cols, cols)
    halos = (
        send(xd.at[jr, pl.ds(0, cols)], next_x, halo_send.at[0], halo_recv.at[0], before),
        send(xd.at[jr, last], prev_x, halo_send.at[1], halo_recv.at[1], after),
        send(gb.at[jr, last], prev_g, halo_send.at[2], halo_recv.at[2], after),
    )

    starts = range(0, cells, step)
    for at in starts:
        here = pl.ds(at, step)
        both, gp, ga = edges(xd[0, here], xd[1, here], gb[2, here], w1[1])
        acc[here] = mm(gp, vw[0])
        sums = weight_sums(gp, ga, both)
        wacc[1] = sums if at == 0 else wacc[1] + sums
    for at in starts:
        here = pl.ds(at, step)
        xu = xd[jc, here]
        wide = xu.astype(F32)
        xv = jnp.concatenate((wide[1:], wide[:1]), 0).astype(BF16)
        both, gp, ga = edges(xu, xv, gb[jc, here], w1[0])
        wide = gp.astype(F32)
        turned = jnp.concatenate((wide[-1:], wide[:-1]), 0).astype(BF16)
        acc[here] += mm(jnp.concatenate((gp, turned), 1), pw[jc])
        sums = weight_sums(gp, ga, both)
        wacc[0] = sums if at == 0 else wacc[0] + sums
    for copy in halos:
        copy.wait()
    _, gp, _ = edges(prev_x[...], xd[jr, pl.ds(0, cols)], prev_g[...], w1[0])
    gps[pl.ds(0, cols)] = gp
    for at in starts:
        here = pl.ds(at, step)
        if at + step < cells:
            xv = xd[jr, pl.ds(at + cols, step)]
        elif step > cols:
            xv = jnp.concatenate((xd[jr, pl.ds(at + cols, step - cols)], next_x[...]), 0)
        else:
            xv = next_x[...]
        both, gp, ga = edges(xd[jr, here], xv, gb[jr, here], w1[0])
        gps[pl.ds(at + cols, step)] = gp
        acc[here] += mm(jnp.concatenate((gp, gps[here]), 1), pw[jr])
        wacc[0] += weight_sums(gp, ga, both)

    def arrived(ref, at):
        wide = ref[:, pl.ds(0, square), :].astype(F32).reshape(strips, rows, rows, ref.shape[2])
        first = at // cols
        parts = [wide[:, r].reshape(cols, ref.shape[2]) for r in range(first, first + chunk)]
        return jnp.concatenate(parts, 0).astype(BF16)

    @pl.when(p < pairs - 1)
    def _():
        wait_bytes(above, cross_recv.at[1])
        for at in starts:
            here = pl.ds(at, step)
            both, gp, ga = edges(xd[1, here], arrived(above, at), gb[3, here], w1[1])
            acc[here] += mm(gp, vw[1])
            wacc[1] += weight_sums(gp, ga, both)

    @pl.when(p > 0)
    def _():
        wait_bytes(below, cross_recv.at[0])
        lanes = below.shape[2]
        tile = below[:, pl.ds(square, TILE), :].astype(F32)
        pick = (
            lax.broadcasted_iota(jnp.int32, (rows, lanes), 0)
            == lax.broadcasted_iota(jnp.int32, (rows, lanes), 1)
        ).astype(F32)
        ones = jnp.ones((lanes, lanes), BF16)
        for at in starts:
            here = pl.ds(at, step)
            first = at // cols
            parts = [
                (tile[:, r : r + 1, :] * pick[None]).reshape(cols, lanes)
                for r in range(first, first + chunk)
            ]
            gate = mm(jnp.concatenate(parts, 0).astype(BF16), ones)
            _, gp, _ = edges(arrived(below, at), xd[0, here], gate, w1[1])
            acc[here] += mm(gp, vw[2])

    feat = wacc.shape[2] // 4
    hidden = wacc.shape[1] // 2
    for kind in range(2):
        g = wacc[kind]
        sd = jnp.concatenate((g[:hidden, :feat], g[:hidden, 2 * feat : 3 * feat]), 1)
        o = g[hidden:, 3 * feat :] - g[hidden:, feat : 2 * feat]
        o = jnp.concatenate((o[: hidden // 2], o[hidden // 2 :]), 1)
        part = jnp.concatenate((sd, o), 0).astype(BF16)
        wpart[pl.ds(kind * (owners // 2), owners // 2)] = part.reshape(owners // 2, TILE, part.shape[1])

    @pl.loop(1, devices)
    def _(k):
        target, to = place(k)

        @pl.when(target < owners)
        def _():
            send(wpart.at[target], wrecv.at[devices - 1 - k], red_send.at[0], red_recv.at[0], to)

    @pl.when(flat < owners)
    def _():
        wait_bytes(wrecv, red_recv.at[0])
        total = jnp.sum(wrecv[...].astype(F32), 0) + wpart[flat].astype(F32)
        wres[flat] = total.astype(BF16)

        @pl.loop(1, devices)
        def _(k):
            send(wres.at[flat], wres.at[flat], red_send.at[1], red_recv.at[1], place(k)[1])

        few = pl.ds(0, owners - 1)
        wait_bytes(wres.at[few], red_recv.at[1])
        wait_bytes(wpart.at[few], red_send.at[0])
        wait_bytes(wrecv, red_send.at[1])

    @pl.when(flat >= owners)
    def _():
        wait_bytes(wres, red_recv.at[1])
        wait_bytes(wpart, red_send.at[0])

    @pl.when(p < pairs - 1)
    def _():
        wait_bytes(s_up, cross_send.at[0])

    @pl.when(p > 0)
    def _():
        wait_bytes(s_dn, cross_send.at[1])

    w_sum[...] = wres[...].astype(F32)


def on_device(nodes, upstream, usage, blockage, capacity, w_src, w_dst, w_out):
    pair = lax.axis_index("lyr")
    strip_at = lax.axis_index("strip")
    pairs = lax.axis_size("lyr")
    strips = lax.axis_size("strip")
    _, layers, feat, rows, cols = nodes.shape
    hidden = w_src.shape[1]
    cells = rows * cols
    damp = lax.rsqrt(1.0 + usage[0].astype(F32))[:, None]
    feats = (nodes[0].astype(F32) * damp).astype(BF16)
    both = jnp.concatenate((feats, upstream[0]), 1)
    xd = jnp.transpose(both, (0, 2, 3, 1)).reshape(layers, cells, 2 * feat)
    turned = jnp.transpose(both, (0, 3, 2, 1)).reshape(layers, strips, rows * rows, 2 * feat)
    gates = (1 - blockage[0]).astype(F32) * capacity[0].astype(F32) * 0.25
    in_rows = (strip_at * rows + jnp.arange(rows) < cols - 1).astype(F32)[:, None]
    in_cols = (jnp.arange(cols) < cols - 1).astype(F32)[None, :]
    first = pair % 2 == 0
    inside = jnp.stack((jnp.where(first, in_rows, in_cols), jnp.where(first, in_cols, in_rows)))
    four = jnp.concatenate((gates[:, 0] * inside, gates[:, 1]), 0).astype(BF16)
    gb = jnp.broadcast_to(four.reshape(4, cells, 1), (4, cells, 2 * feat))
    tile = jnp.transpose(gates[1, 1].astype(BF16).reshape(rows, strips, rows), (1, 2, 0))
    tile = jnp.pad(tile, ((0, 0), (0, TILE - rows), (0, 2 * feat - rows)))
    s_up = jnp.concatenate((turned[1], tile), 1)
    s_dn = turned[0]

    zero = jnp.zeros((2, feat, hidden), BF16)
    w1 = jnp.concatenate(
        (
            jnp.concatenate((jnp.swapaxes(w_src, 1, 2), zero), 2),
            jnp.concatenate((zero, -w_out), 2),
            jnp.concatenate((jnp.swapaxes(w_dst, 1, 2), zero), 2),
            jnp.concatenate((zero, w_out), 2),
        ),
        1,
    )
    blank = jnp.zeros((2 * hidden, feat), BF16)
    planar = jnp.concatenate((w_src[0], w_dst[0]), 0)
    pw = jnp.stack((jnp.concatenate((planar, blank), 1), jnp.concatenate((blank, planar), 1)))
    none = jnp.zeros((hidden, feat), BF16)
    vw = jnp.stack(
        (
            jnp.concatenate((w_src[1], w_dst[1]), 1),
            jnp.concatenate((none, w_src[1]), 1),
            jnp.concatenate((w_dst[1], none), 1),
        )
    )
    lanes = 2 * feat
    owners = 2 * 3 * hidden * feat // (TILE * lanes)
    devices = pairs * strips
    chunk = max(1, min(rows, 1024 // cols))
    vmem = pl.BlockSpec(memory_space=pltpu.VMEM)
    acc, w_sum = pl.pallas_call(
        functools.partial(kernel, pairs, strips, rows, cols, chunk),
        out_shape=(
            jax.ShapeDtypeStruct((cells, lanes), F32),
            jax.ShapeDtypeStruct((owners, TILE, lanes), F32),
        ),
        in_specs=[vmem] * 7,
        out_specs=(vmem, vmem),
        scratch_shapes=[
            pltpu.VMEM((cols, lanes), BF16),
            pltpu.VMEM((cols, lanes), BF16),
            pltpu.VMEM((cols, lanes), BF16),
            pltpu.VMEM((strips, rows * rows + TILE, lanes), BF16),
            pltpu.VMEM((strips, rows * rows, lanes), BF16),
            pltpu.VMEM((cells + cols, hidden), BF16),
            pltpu.VMEM((2, 2 * hidden, 4 * feat), F32),
            pltpu.VMEM((owners, TILE, lanes), BF16),
            pltpu.VMEM((devices - 1, TILE, lanes), BF16),
            pltpu.VMEM((owners, TILE, lanes), BF16),
            pltpu.SemaphoreType.DMA((3,)),
            pltpu.SemaphoreType.DMA((3,)),
            pltpu.SemaphoreType.DMA((2,)),
            pltpu.SemaphoreType.DMA((2,)),
            pltpu.SemaphoreType.DMA((2,)),
            pltpu.SemaphoreType.DMA((2,)),
        ],
        compiler_params=pltpu.CompilerParams(
            collective_id=0, has_side_effects=True, vmem_limit_bytes=48 * 1024 * 1024
        ),
    )(xd, s_up, s_dn, gb, w1, pw, vw)

    node_sum = jnp.transpose(acc.reshape(rows, cols, layers, feat), (2, 3, 0, 1))
    grad_nodes = (upstream[0].astype(F32) + damp * node_sum).astype(BF16)[None]
    scale = 1.0 / math.sqrt(2 * pairs * cols * cols)
    w_sum = w_sum.reshape(2, 3 * hidden // 2, lanes) * scale
    g_src = w_sum[:, :hidden, :feat]
    g_dst = w_sum[:, :hidden, feat:]
    out = w_sum[:, hidden:]
    g_out = jnp.swapaxes(jnp.concatenate((out[:, :, :feat], out[:, :, feat:]), 1), 1, 2)
    return grad_nodes, g_src, g_dst, g_out


def solution(mesh):
    placed = (
        P("lyr", None, None, "strip", None),
        P("lyr", None, None, "strip", None),
        P("lyr", None, "strip", None),
        P("lyr", None, None, "strip", None),
        P("lyr", None, None, "strip", None),
        P(),
        P(),
        P(),
    )
    return jax.shard_map(
        on_device,
        mesh=mesh,
        in_specs=placed,
        out_specs=(P("lyr", None, None, "strip", None), P(), P(), P()),
        check_vma=False,
    )
```

time: 221 us -> 39.3 us (0.18); the launches traced: 218 us -> 38.8 us
  waiting for transfers between devices: 120 us -> 0 us
  Pallas kernels: 0 us -> 27.2 us
  starting transfers between devices: 23.7 us -> 0 us
  local copies, waits for them, and re-layouts: 31.4 us -> 8.81 us
  matrix products: 16.6 us -> 0 us
  between operations: 14.9 us -> 0.89 us
  other arithmetic: 11.7 us -> 1.91 us
    psum x1 -> x0, waiting for transfers between devices: 119 us -> none  [on_device(): joined = lax.psum((joined[0], joined[1], joined[2]), ('lyr', 'strip'))]
    pallas_call x0 -> x1, Pallas kernels: none -> 27.2 us  [on_device(): pl.pallas_call(functools.partial(kernel, pairs, strips, rows, cols, chunk...]
    dot_general x32 -> x0, matrix products: 16.6 us -> none  [the longest x4 3.51 us: edge_grads(): lax.dot_general(g_msg, act, (((1,), (1,)), ((), ())), preferred_element_t...]
    all_to_all x2 -> x0, starting transfers between devices: 15.1 us -> none  [the longest x1 10.1 us: on_device(): lax.all_to_all(packed, 'strip', split_axis=3, concat_axis=2, tiled=True)]
    unnamed x146 -> x28, local copies, waits for them, and re-layouts: 18.1 us -> 6.65 us
    ppermute x4 -> x0, starting transfers between devices: 8.63 us -> none  [from_behind(): lax.ppermute(value, axis, [(source, source + steps) for source in range(i...]
    mul x7 -> x1, other arithmetic: 4.74 us -> 0.01 us  [on_device(): w_sum = w_sum.reshape(2, 3 * hidden // 2, lanes) * scale]
    convert_element_type x8 -> x3, other arithmetic: 3.32 us -> 0.06 us  [the longest x1 0.05 us: on_device(): feats = (nodes[0].astype(F32) * damp).astype(BF16)]
  transfers between devices with their start and end apart: 7 -> 0, of which waited for: 2 -> 0; matrix products, arithmetic and copies ran while one was open for 16% -> 0% of each run, Pallas kernels for 0% -> 0%
where the time goes in v1:
time: 39.3 us; the launch traced here: 38.8 us
  Pallas kernels  27.2 us (69%)
  local copies, waits for them, and re-layouts  8.81 us (22%)
  other arithmetic  1.91 us (5%)
  between operations  0.89 us (2%)
    pallas_call x1, Pallas kernels, on_device(): pl.pallas_call(functools.partial(kernel, pairs, strips, rows, cols, chunk...  27.2 us
    unnamed x28, local copies, waits for them, and re-layouts  6.65 us

profile of v1, /device:TPU:0, one launch (start us, length us, event | category | flops | bytes accessed | tf_op | source)
XLA Modules:
  0.0 38.8 jit_solution(11015683770679342234)
XLA Ops:
  0.7 0.0 copy-start.7
  0.7 0.1 broadcast_in_dim.50
  0.8 0.0 copy-start.5
  0.8 0.0 copy-start.6
  0.8 0.6 %copy-done.7 = s32[1,2,8,128]{3,2,1,0:T(8,128)S(1)} copy-done((s32[1,2,8,128]{3,2,1,0:T(8,128)S(1)}, s32[1,2,8,128]{3,2,1,0:T(8,128)}, u32[]{:S(2)}) %copy-start.7) | copy-done | bytes 8216
  1.4 0.1 copy-done.5
  1.5 0.0 copy-done.6
  1.6 0.0 copy-start.2
  1.6 0.1 copy.27
  1.7 0.6 %copy-done.2 = bf16[2,64,128]{2,1,0:T(8,128)(2,1)S(1)} copy-done((bf16[2,64,128]{2,1,0:T(8,128)(2,1)S(1)}, bf16[2,64,128]{2,1,0:T(8,128)(2,1)}, u32[]{:S(2)}) %copy-start.2) | copy-done | bytes 32792
  2.3 0.0 copy-start.4
  2.3 0.7 %copy-done.4 = bf16[2,128,64]{1,2,0:T(8,128)(2,1)S(1)} copy-done((bf16[2,128,64]{1,2,0:T(8,128)(2,1)S(1)}, bf16[2,128,64]{1,2,0:T(8,128)(2,1)}, u32[]{:S(2)}) %copy-start.4) | copy-done | bytes 32792
  3.1 0.1 copy.40
  3.2 0.0 copy-start.3
  3.2 0.1 copy.38
  3.3 0.6 %copy-done.3 = bf16[2,128,64]{1,2,0:T(8,128)(2,1)S(1)} copy-done((bf16[2,128,64]{1,2,0:T(8,128)(2,1)S(1)}, bf16[2,128,64]{1,2,0:T(8,128)(2,1)}, u32[]{:S(2)}) %copy-start.3) | copy-done | bytes 32792
  4.0 0.1 copy.41
  4.1 0.1 copy.39
  4.2 0.1 maximum_bitcast_fusion.1
  4.4 0.1 pad_bitcast_fusion.1
  4.5 0.0 copy-start.1
  4.5 0.9 %copy-done.1 = bf16[1,2,64,8,128]{4,3,2,1,0:T(8,128)(2,1)S(1)} copy-done((bf16[1,2,64,8,128]{4,3,2,1,0:T(8,128)(2,1)S(1)}, bf16[1,2,64,8,128]{4,3,2,1,0:T(8,128)(2,1)}, u32[]{:S(2)}) %copy-start.1) | copy-done | bytes 262168
  5.4 0.0 copy-start
  5.4 0.1 fusion.1
  5.5 0.9 %copy-done = bf16[1,2,64,8,128]{4,3,2,1,0:T(8,128)(2,1)S(1)} copy-done((bf16[1,2,64,8,128]{4,3,2,1,0:T(8,128)(2,1)S(1)}, bf16[1,2,64,8,128]{4,3,2,1,0:T(8,128)(2,1)}, u32[]{:S(2)}) %copy-start) | copy-done | bytes 262168
  6.4 0.1 fusion.10
  6.5 0.2 copy.28
  6.7 0.2 copy.26
  7.0 0.4 copy.25
  7.4 0.6 %broadcast_in_dim.54.gb = bf16[4,1024,128]{2,1,0:T(8,128)(2,1)S(1)} broadcast(bf16[4,1024]{1,0:T(4,128)(2,1)S(1)} %pad_maximum_fusion.4), dimensions={0,1} | broadcast | bytes 1056768 | tf_op jit(solution)/shard_map/broadcast_in_dim | solution.py:239
  8.0 27.2 %shard_map.111 = (f32[1024,128]{1,0:T(8,128)S(1)}, f32[24,16,128]{2,1,0:T(8,128)S(1)}) custom-call(bf16[2,1024,128]{2,1,0:T(8,128)(2,1)S(1)} %bitcast.69, bf16[16,80,128]{2,1,0:T(8,128)(2,1)S(1)} %fusion.12.s_up, bf16[16,64,128]{2,1,0:T(8,128)(2,1)S(1)} %bitcast.70, bf16[4,1024,128]{2,1,0:T(8,128)(2,1)S(1)} %broadcast_in_dim.54.gb, ...), custom_call_target="tpu_custom_call" | custom-call | tf_op jit(solution)/shard_map/pallas_call | solution.py:271
  35.2 0.2 copy.33
  35.4 0.1 copy.48
  35.5 0.8 %fusion.16 = bf16[1,2,64,8,128]{4,3,2,1,0:T(8,128)(2,1)} fusion(f32[8,128,2,64]{1,0,3,2:T(8,128)S(1)} %bitcast.71, f32[2,8,128]{2,1,0:T(8,128)S(1)} %rsqrt_bitcast_fusion, bf16[1,2,64,8,128]{4,3,2,1,0:T(8,128)(2,1)S(1)} %copy-done), kind=kLoop, calls=%fused_computation.26 | loop fusion | flops 524288 | bytes 1056768 | tf_op jit(solution)/shard_map/broadcast_in_dim | solution.py:303
  36.3 0.1 fusion.20
  36.4 0.1 copy.44
  36.5 0.1 copy.45
  36.6 0.7 %maximum_bitcast_fusion = f32[2,64,128]{2,1,0:T(8,128)} fusion(f32[2,64,64]{1,2,0:T(8,128)S(1)} %copy.45, f32[2,64,64]{1,2,0:T(8,128)S(1)} %copy.44), kind=kLoop, calls=%fused_computation.31 | loop fusion | flops 16384 | bytes 131072 | tf_op jit(solution)/shard_map/transpose | solution.py:309
  37.3 0.1 fusion.21
  37.4 0.7 %copy.43 = f32[2,128,64]{1,2,0:T(8,128)} copy(f32[2,128,64]{2,1,0:T(8,128)S(1)} %get-tuple-element.16) | data formatting | bytes 131072
  38.1 0.7 %copy.42 = f32[2,128,64]{1,2,0:T(8,128)} copy(f32[2,128,64]{2,1,0:T(8,128)S(1)} %get-tuple-element.17) | data formatting | bytes 131072
  (22 shorter events, 0.3 us)
Async XLA Ops:
  0.7 0.7 %copy-start.7 = (s32[1,2,8,128]{3,2,1,0:T(8,128)S(1)}, s32[1,2,8,128]{3,2,1,0:T(8,128)}, u32[]{:S(2)}) copy-start(s32[1,2,8,128]{3,2,1,0:T(8,128)} %param.10) | copy-start | bytes 24580
  0.8 0.7 %copy-start.5 = (s32[1,2,2,8,128]{4,3,2,1,0:T(8,128)S(1)}, s32[1,2,2,8,128]{4,3,2,1,0:T(8,128)}, u32[]{:S(2)}) copy-start(s32[1,2,2,8,128]{4,3,2,1,0:T(8,128)} %param.12) | copy-start | bytes 49156
  0.8 0.7 %copy-start.6 = (s32[1,2,2,8,128]{4,3,2,1,0:T(8,128)S(1)}, s32[1,2,2,8,128]{4,3,2,1,0:T(8,128)}, u32[]{:S(2)}) copy-start(s32[1,2,2,8,128]{4,3,2,1,0:T(8,128)} %param.11) | copy-start | bytes 49156
  1.6 0.8 %copy-start.2 = (bf16[2,64,128]{2,1,0:T(8,128)(2,1)S(1)}, bf16[2,64,128]{2,1,0:T(8,128)(2,1)}, u32[]{:S(2)}) copy-start(bf16[2,64,128]{2,1,0:T(8,128)(2,1)} %param.15) | copy-start | bytes 98308
  2.3 0.8 %copy-start.4 = (bf16[2,128,64]{1,2,0:T(8,128)(2,1)S(1)}, bf16[2,128,64]{1,2,0:T(8,128)(2,1)}, u32[]{:S(2)}) copy-start(bf16[2,128,64]{1,2,0:T(8,128)(2,1)} %param.13) | copy-start | bytes 98308
  3.2 0.8 %copy-start.3 = (bf16[2,128,64]{1,2,0:T(8,128)(2,1)S(1)}, bf16[2,128,64]{1,2,0:T(8,128)(2,1)}, u32[]{:S(2)}) copy-start(bf16[2,128,64]{1,2,0:T(8,128)(2,1)} %param.14) | copy-start | bytes 98308
  4.5 1.0 %copy-start.1 = (bf16[1,2,64,8,128]{4,3,2,1,0:T(8,128)(2,1)S(1)}, bf16[1,2,64,8,128]{4,3,2,1,0:T(8,128)(2,1)}, u32[]{:S(2)}) copy-start(bf16[1,2,64,8,128]{4,3,2,1,0:T(8,128)(2,1)} %param.8) | copy-start | bytes 786436
  5.4 0.9 %copy-start = (bf16[1,2,64,8,128]{4,3,2,1,0:T(8,128)(2,1)S(1)}, bf16[1,2,64,8,128]{4,3,2,1,0:T(8,128)(2,1)}, u32[]{:S(2)}) copy-start(bf16[1,2,64,8,128]{4,3,2,1,0:T(8,128)(2,1)} %param.9) | copy-start | bytes 786436

commit v2 on v1

--- a/solution.py
+++ b/solution.py
@@ -37,8 +37,10 @@
 
 def kernel(
     pairs, strips, rows, cols, chunk,
+    nodes, up, usage, blockage, capacity, w_src, w_dst, w_out,
+    acc, w_sum,
     xd, s_up, s_dn, gb, w1, pw, vw,
-    acc, w_sum,
+    nv, uv, usv, bv, cv, wsv, wdv, wov, t_rows, q_rows, in_sems,
     prev_x, next_x, prev_g, below, above, gps, wacc, wpart, wrecv, wres,
     halo_send, halo_recv, cross_send, cross_recv, red_send, red_recv,
 ):
@@ -61,6 +63,12 @@
     def _(k):
         pl.semaphore_signal(barrier, inc=1, device_id=place(k)[1], device_id_type=MESH)
 
+    stage(
+        pairs, strips,
+        nodes, up, usage, blockage, capacity, w_src, w_dst, w_out,
+        xd, s_up, s_dn, gb, w1, pw, vw,
+        nv, uv, usv, bv, cv, wsv, wdv, wov, t_rows, q_rows, in_sems,
+    )
     pl.semaphore_wait(barrier, devices - 1)
 
     jr = lax.rem(p, 2)
@@ -75,18 +83,6 @@
 
     def wait_bytes(ref, sem):
         pltpu.make_async_copy(ref, ref, sem).wait()
-
-    @pl.loop(0, strips)
-    def _(k):
-        t = lax.rem(s + k, strips)
-
-        @pl.when(p < pairs - 1)
-        def _():
-            send(s_up.at[t], below.at[s], cross_send.at[0], cross_recv.at[0], (p + 1, t))
-
-        @pl.when(p > 0)
-        def _():
-            send(s_dn.at[t], above.at[s], cross_send.at[1], cross_recv.at[1], (p - 1, t))
 
     after = (p, lax.rem(s + 1, strips))
     before = (p, lax.rem(s + strips - 1, strips))
@@ -96,6 +92,18 @@
         send(xd.at[jr, last], prev_x, halo_send.at[1], halo_recv.at[1], after),
         send(gb.at[jr, last], prev_g, halo_send.at[2], halo_recv.at[2], after),
     )
+
+    @pl.loop(0, strips)
+    def _(k):
+        t = lax.rem(s + k, strips)
+
+        @pl.when(p < pairs - 1)
+        def _():
+            send(s_up.at[t], below.at[s], cross_send.at[0], cross_recv.at[0], (p + 1, t))
+
+        @pl.when(p > 0)
+        def _():
+            send(s_dn.at[t], above.at[s], cross_send.at[1], cross_recv.at[1], (p - 1, t))
 
     starts = range(0, cells, step)
     for at in starts:
@@ -132,6 +140,28 @@
         acc[here] += mm(jnp.concatenate((gp, gps[here]), 1), pw[jr])
         wacc[0] += weight_sums(gp, ga, both)
 
+    feat = wacc.shape[2] // 4
+    hidden = wacc.shape[1] // 2
+
+    def reduce_out(kind):
+        half = owners // 2
+        g = wacc[kind]
+        sd = jnp.concatenate((g[:hidden, :feat], g[:hidden, 2 * feat : 3 * feat]), 1)
+        o = g[hidden:, 3 * feat :] - g[hidden:, feat : 2 * feat]
+        o = jnp.concatenate((o[: hidden // 2], o[hidden // 2 :]), 1)
+        part = jnp.concatenate((sd, o), 0).astype(BF16)
+        wpart[pl.ds(kind * half, half)] = part.reshape(half, TILE, part.shape[1])
+
+        @pl.loop(1, devices)
+        def _(k):
+            target, to = place(k)
+
+            @pl.when((target >= kind * half) & (target < (kind + 1) * half))
+            def _():
+                send(wpart.at[target], wrecv.at[devices - 1 - k], red_send.at[0], red_recv.at[0], to)
+
+    reduce_out(0)
+
     def arrived(ref, at):
         wide = ref[:, pl.ds(0, square), :].astype(F32).reshape(strips, rows, rows, ref.shape[2])
         first = at // cols
@@ -168,23 +198,7 @@
             _, gp, _ = edges(arrived(below, at), xd[0, here], gate, w1[1])
             acc[here] += mm(gp, vw[2])
 
-    feat = wacc.shape[2] // 4
-    hidden = wacc.shape[1] // 2
-    for kind in range(2):
-        g = wacc[kind]
-        sd = jnp.concatenate((g[:hidden, :feat], g[:hidden, 2 * feat : 3 * feat]), 1)
-        o = g[hidden:, 3 * feat :] - g[hidden:, feat : 2 * feat]
-        o = jnp.concatenate((o[: hidden // 2], o[hidden // 2 :]), 1)
-        part = jnp.concatenate((sd, o), 0).astype(BF16)
-        wpart[pl.ds(kind * (owners // 2), owners // 2)] = part.reshape(owners // 2, TILE, part.shape[1])
-
-    @pl.loop(1, devices)
-    def _(k):
-        target, to = place(k)
-
-        @pl.when(target < owners)
-        def _():
-            send(wpart.at[target], wrecv.at[devices - 1 - k], red_send.at[0], red_recv.at[0], to)
+    reduce_out(1)
 
     @pl.when(flat < owners)
     def _():
@@ -217,66 +231,177 @@
     w_sum[...] = wres[...].astype(F32)
 
 
+LANES = 128
+
+
+def fetch(pairs_of_refs, sems):
+    copies = [pltpu.make_async_copy(a, b, sems.at[i]) for i, (a, b) in enumerate(pairs_of_refs)]
+    for copy in copies:
+        copy.start()
+    for copy in copies:
+        copy.wait()
+
+
+def stage(
+    pairs, strips,
+    nodes, up, usage, blockage, capacity, w_src, w_dst, w_out,
+    xd, s_up, s_dn, gb, w1, pw, vw,
+    nv, uv, usv, bv, cv, wsv, wdv, wov, t, q, sems,
+):
+    p = lax.axis_index("lyr")
+    s = lax.axis_index("strip")
+    fetch(
+        (
+            (nodes, nv), (up, uv), (usage, usv), (blockage, bv), (capacity, cv),
+            (w_src, wsv), (w_dst, wdv), (w_out, wov),
+        ),
+        sems,
+    )
+    _, layers, feat, rows, cols = nv.shape
+    lanes = 2 * feat
+    half = feat * rows
+    blocks = cols // LANES
+    damp = lax.rsqrt(1.0 + usv[0].astype(F32))
+    for j in range(layers):
+        x = (nv[0, j].astype(F32) * damp[j][None]).astype(BF16).astype(F32)
+        d = uv[0, j].astype(F32)
+        for b in range(blocks):
+            cut = slice(b * LANES, (b + 1) * LANES)
+            t[b, pl.ds(0, half)] = x[:, :, cut].reshape(half, LANES)
+            t[b, pl.ds(half, half)] = d[:, :, cut].reshape(half, LANES)
+        for r in range(rows):
+            for b in range(blocks):
+                m = t[b, pl.ds(r, lanes, stride=rows), :]
+                xd[j, pl.ds(r * cols + b * LANES, LANES)] = m.T.astype(BF16)
+
+    def spread(j, out):
+        for r in range(rows):
+            q[pl.ds(r, cols, stride=rows), :] = xd[j, pl.ds(r * cols, cols)].astype(F32)
+        out[:, pl.ds(0, rows * rows), :] = q[...].astype(BF16).reshape(strips, rows * rows, lanes)
+
+    @pl.when(p > 0)
+    def _():
+        spread(0, s_dn)
+
+    gates = (1 - bv[0]).astype(F32) * cv[0].astype(F32) * 0.25
+
+    @pl.when(p < pairs - 1)
+    def _():
+        spread(1, s_up)
+        per = LANES // rows
+        for b in range(blocks):
+            g = gates[1, 1][:, b * LANES : (b + 1) * LANES]
+            g = jnp.concatenate((g, jnp.zeros((LANES - rows, LANES), F32)), 0).T.reshape(per, rows, LANES)
+            g = jnp.concatenate((g, jnp.zeros((per, TILE - rows, LANES), F32)), 1)
+            s_up[pl.ds(b * per, per), pl.ds(rows * rows, TILE), :] = g.astype(BF16)
+
+    row_ids = s * rows + lax.broadcasted_iota(jnp.int32, (rows, cols), 0)
+    in_rows = (row_ids < cols - 1).astype(F32)
+    in_cols = (lax.broadcasted_iota(jnp.int32, (rows, cols), 1) < cols - 1).astype(F32)
+    odd = lax.rem(p, 2).astype(F32)
+    low = (1.0 - odd) * in_rows + odd * in_cols
+    high = odd * in_rows + (1.0 - odd) * in_cols
+    four = (gates[0, 0] * low, gates[1, 0] * high, gates[0, 1], gates[1, 1])
+    eye = (
+        lax.broadcasted_iota(jnp.int32, (LANES, LANES), 0)
+        == lax.broadcasted_iota(jnp.int32, (LANES, LANES), 1)
+    ).astype(F32)
+    ones = jnp.ones((LANES, lanes), BF16)
+    for k, g in enumerate(four):
+        parts = [
+            (eye * g[r : r + 1, b * LANES : (b + 1) * LANES]).astype(BF16)
+            for r in range(rows)
+            for b in range(blocks)
+        ]
+        gb[k] = mm(jnp.concatenate(parts, 0), ones).astype(BF16)
+
+    hidden = wsv.shape[2]
+    zero = jnp.zeros((feat, hidden), BF16)
+    for k in range(2):
+        wo = wov[k]
+        less = (-wo.astype(F32)).astype(BF16)
+        w1[k, pl.ds(0, feat)] = jnp.concatenate((wsv[k], zero), 1)
+        w1[k, pl.ds(feat, feat)] = jnp.concatenate((zero, less), 1)
+        w1[k, pl.ds(2 * feat, feat)] = jnp.concatenate((wdv[k], zero), 1)
+        w1[k, pl.ds(3 * feat, feat)] = jnp.concatenate((zero, wo), 1)
+    none = jnp.zeros((hidden, feat), BF16)
+    src, dst = [[v[k].astype(F32).T.astype(BF16) for k in range(2)] for v in (wsv, wdv)]
+    for i, w in enumerate((src, dst)):
+        here = pl.ds(i * hidden, hidden)
+        pw[0, here] = jnp.concatenate((w[0], none), 1)
+        pw[1, here] = jnp.concatenate((none, w[0]), 1)
+    vw[0] = jnp.concatenate((src[1], dst[1]), 1)
+    vw[1] = jnp.concatenate((none, src[1]), 1)
+    vw[2] = jnp.concatenate((dst[1], none), 1)
+
+
+def finish(scale, acc_in, w_in, up, usage, gn, gs, gd, go, acc, w_sum, uv, usv, t, sems):
+    fetch(((acc_in, acc), (w_in, w_sum), (up, uv), (usage, usv)), sems)
+    _, layers, feat, rows, cols = uv.shape
+    lanes = 2 * feat
+    half = feat * rows
+    blocks = cols // LANES
+    for b in range(blocks):
+        for r in range(rows):
+            t[b, pl.ds(r, lanes, stride=rows), :] = acc[pl.ds(r * cols + b * LANES, LANES)].T
+    damp = lax.rsqrt(1.0 + usv[0].astype(F32))
+    for j in range(layers):
+        for b in range(blocks):
+            cut = pl.ds(b * LANES, LANES)
+            ns = t[b, pl.ds(j * half, half)].reshape(feat, rows, LANES)
+            scaled = damp[j][None, :, b * LANES : (b + 1) * LANES] * ns
+            gn[0, j, :, :, cut] = (uv[0, j, :, :, cut].astype(F32) + scaled).astype(BF16)
+    hidden = gs.shape[2]
+    w = w_sum[...].reshape(2, 3 * hidden // 2, lanes) * scale
+    for k in range(2):
+        sd = w[k, :hidden].T
+        gs[k] = sd[:feat]
+        gd[k] = sd[feat:]
+        o = w[k, hidden:]
+        go[k] = jnp.concatenate((o[:, :feat], o[:, feat:]), 0).T
+
+
 def on_device(nodes, upstream, usage, blockage, capacity, w_src, w_dst, w_out):
-    pair = lax.axis_index("lyr")
-    strip_at = lax.axis_index("strip")
     pairs = lax.axis_size("lyr")
     strips = lax.axis_size("strip")
     _, layers, feat, rows, cols = nodes.shape
     hidden = w_src.shape[1]
     cells = rows * cols
-    damp = lax.rsqrt(1.0 + usage[0].astype(F32))[:, None]
-    feats = (nodes[0].astype(F32) * damp).astype(BF16)
-    both = jnp.concatenate((feats, upstream[0]), 1)
-    xd = jnp.transpose(both, (0, 2, 3, 1)).reshape(layers, cells, 2 * feat)
-    turned = jnp.transpose(both, (0, 3, 2, 1)).reshape(layers, strips, rows * rows, 2 * feat)
-    gates = (1 - blockage[0]).astype(F32) * capacity[0].astype(F32) * 0.25
-    in_rows = (strip_at * rows + jnp.arange(rows) < cols - 1).astype(F32)[:, None]
-    in_cols = (jnp.arange(cols) < cols - 1).astype(F32)[None, :]
-    first = pair % 2 == 0
-    inside = jnp.stack((jnp.where(first, in_rows, in_cols), jnp.where(first, in_cols, in_rows)))
-    four = jnp.concatenate((gates[:, 0] * inside, gates[:, 1]), 0).astype(BF16)
-    gb = jnp.broadcast_to(four.reshape(4, cells, 1), (4, cells, 2 * feat))
-    tile = jnp.transpose(gates[1, 1].astype(BF16).reshape(rows, strips, rows), (1, 2, 0))
-    tile = jnp.pad(tile, ((0, 0), (0, TILE - rows), (0, 2 * feat - rows)))
-    s_up = jnp.concatenate((turned[1], tile), 1)
-    s_dn = turned[0]
-
-    zero = jnp.zeros((2, feat, hidden), BF16)
-    w1 = jnp.concatenate(
-        (
-            jnp.concatenate((jnp.swapaxes(w_src, 1, 2), zero), 2),
-            jnp.concatenate((zero, -w_out), 2),
-            jnp.concatenate((jnp.swapaxes(w_dst, 1, 2), zero), 2),
-            jnp.concatenate((zero, w_out), 2),
-        ),
-        1,
-    )
-    blank = jnp.zeros((2 * hidden, feat), BF16)
-    planar = jnp.concatenate((w_src[0], w_dst[0]), 0)
-    pw = jnp.stack((jnp.concatenate((planar, blank), 1), jnp.concatenate((blank, planar), 1)))
-    none = jnp.zeros((hidden, feat), BF16)
-    vw = jnp.stack(
-        (
-            jnp.concatenate((w_src[1], w_dst[1]), 1),
-            jnp.concatenate((none, w_src[1]), 1),
-            jnp.concatenate((w_dst[1], none), 1),
-        )
-    )
     lanes = 2 * feat
     owners = 2 * 3 * hidden * feat // (TILE * lanes)
     devices = pairs * strips
     chunk = max(1, min(rows, 1024 // cols))
     vmem = pl.BlockSpec(memory_space=pltpu.VMEM)
+    hbm = pl.BlockSpec(memory_space=pltpu.HBM)
+    params = pltpu.CompilerParams(vmem_limit_bytes=63 * 1024 * 1024)
+    given = (nodes, upstream, usage, blockage, capacity)
+    given += (jnp.swapaxes(w_src, 1, 2), jnp.swapaxes(w_dst, 1, 2), w_out)
+
+    def shape(dims, kind=BF16):
+        return jax.ShapeDtypeStruct(dims, kind)
+
     acc, w_sum = pl.pallas_call(
         functools.partial(kernel, pairs, strips, rows, cols, chunk),
         out_shape=(
             jax.ShapeDtypeStruct((cells, lanes), F32),
             jax.ShapeDtypeStruct((owners, TILE, lanes), F32),
         ),
-        in_specs=[vmem] * 7,
+        in_specs=[hbm] * 8,
         out_specs=(vmem, vmem),
         scratch_shapes=[
+            pltpu.VMEM((layers, cells, lanes), BF16),
+            pltpu.VMEM((strips, rows * rows + TILE, lanes), BF16),
+            pltpu.VMEM((strips, rows * rows, lanes), BF16),
+            pltpu.VMEM((4, cells, lanes), BF16),
+            pltpu.VMEM((2, 4 * feat, 2 * hidden), BF16),
+            pltpu.VMEM((2, 2 * hidden, lanes), BF16),
+            pltpu.VMEM((3, hidden, lanes), BF16),
+        ]
+        + [pltpu.VMEM(a.shape, a.dtype) for a in given]
+        + [
+            pltpu.VMEM((cols // LANES, lanes * rows, LANES), F32),
+            pltpu.VMEM((cells, lanes), F32),
+            pltpu.SemaphoreType.DMA((8,)),
             pltpu.VMEM((cols, lanes), BF16),
             pltpu.VMEM((cols, lanes), BF16),
             pltpu.VMEM((cols, lanes), BF16),
@@ -295,19 +420,32 @@
             pltpu.SemaphoreType.DMA((2,)),
         ],
         compiler_params=pltpu.CompilerParams(
-            collective_id=0, has_side_effects=True, vmem_limit_bytes=48 * 1024 * 1024
+            collective_id=0, has_side_effects=True, vmem_limit_bytes=63 * 1024 * 1024
         ),
-    )(xd, s_up, s_dn, gb, w1, pw, vw)
-
-    node_sum = jnp.transpose(acc.reshape(rows, cols, layers, feat), (2, 3, 0, 1))
-    grad_nodes = (upstream[0].astype(F32) + damp * node_sum).astype(BF16)[None]
+    )(*given)
+
     scale = 1.0 / math.sqrt(2 * pairs * cols * cols)
-    w_sum = w_sum.reshape(2, 3 * hidden // 2, lanes) * scale
-    g_src = w_sum[:, :hidden, :feat]
-    g_dst = w_sum[:, :hidden, feat:]
-    out = w_sum[:, hidden:]
-    g_out = jnp.swapaxes(jnp.concatenate((out[:, :, :feat], out[:, :, feat:]), 1), 1, 2)
-    return grad_nodes, g_src, g_dst, g_out
+    gn, gs, gd, go = pl.pallas_call(
+        functools.partial(finish, scale),
+        out_shape=(
+            shape(nodes.shape),
+            shape((2, feat, hidden), F32),
+            shape((2, feat, hidden), F32),
+            shape(w_out.shape, F32),
+        ),
+        in_specs=[hbm] * 4,
+        out_specs=(vmem,) * 4,
+        scratch_shapes=[
+            pltpu.VMEM(acc.shape, acc.dtype),
+            pltpu.VMEM(w_sum.shape, w_sum.dtype),
+            pltpu.VMEM(upstream.shape, upstream.dtype),
+            pltpu.VMEM(usage.shape, usage.dtype),
+            pltpu.VMEM((cols // LANES, lanes * rows, LANES), F32),
+            pltpu.SemaphoreType.DMA((4,)),
+        ],
+        compiler_params=params,
+    )(acc, w_sum, upstream, usage)
+    return gn, jnp.swapaxes(gs, 1, 2), jnp.swapaxes(gd, 1, 2), go
 
 
 def solution(mesh):

time: 39.3 us -> 29.8 us (0.76)
  local copies, waits for them, and re-layouts: 8.81 us -> 0 us
  other arithmetic: 1.91 us -> 0 us
  Pallas kernels: 27.2 us -> 29 us
    unnamed x28 -> x0, local copies, waits for them, and re-layouts: 6.65 us -> none
    pallas_call x0 -> x1, Pallas kernels: none -> 2.25 us  [on_device(): pl.pallas_call(functools.partial(finish, scale), out_shape=(shape(nodes.s...]
    slice x9 -> x0, local copies, waits for them, and re-layouts: 0.82 us -> none  [the longest x2 0.28 us: on_device(): s_dn = turned[0]]
    transpose x2 -> x0, other arithmetic: 0.79 us -> none  [the longest x1 0.72 us: on_device(): jnp.swapaxes(jnp.concatenate((out[:, :, :feat], out[:, :, feat:]), 1), 1, 2)]
    broadcast_in_dim x1 -> x0, other arithmetic: 0.78 us -> none  [on_device(): grad_nodes = (upstream[0].astype(F32) + damp * node_sum).astype(BF16)[None]]
    broadcast_in_dim x3 -> x0, local copies, waits for them, and re-layouts: 0.68 us -> none  [the longest x1 0.61 us: on_device(): gb = jnp.broadcast_to(four.reshape(4, cells, 1), (4, cells, 2 * feat))]
    pallas_call x1, Pallas kernels: 27.2 us -> 26.8 us  [on_device(): pl.pallas_call(functools.partial(kernel, pairs, strips, rows, cols, chunk...]
where the time goes in v2:
time: 29.8 us; the launch traced here: 29.7 us
  Pallas kernels  29 us (97%)
  between operations  0.64 us (2%)
    pallas_call x1, Pallas kernels, on_device(): pl.pallas_call(functools.partial(kernel, pairs, strips, rows, cols, chunk...  26.8 us
    pallas_call x1, Pallas kernels, on_device(): pl.pallas_call(functools.partial(finish, scale), out_shape=(shape(nodes.s...  2.25 us

profile of v2, /device:TPU:0, one launch (start us, length us, event | category | flops | bytes accessed | tf_op | source)
XLA Modules:
  0.0 29.7 jit_solution(3330102463530376766)
XLA Ops:
  0.6 26.8 %shard_map.111 = (f32[1024,128]{1,0:T(8,128)}, f32[24,16,128]{2,1,0:T(8,128)}) custom-call(bf16[1,2,64,8,128]{4,3,2,1,0:T(8,128)(2,1)} %nodes.1, bf16[1,2,64,8,128]{4,3,2,1,0:T(8,128)(2,1)} %up.3, s32[1,2,8,128]{3,2,1,0:T(8,128)} %usage.3, s32[1,2,2,8,128]{4,3,2,1,0:T(8,128)} %blockage.1, s32[1,2,2,8,128]{4,3,2,1,0:T(8,128)} %capacity.1, ...), custom_call_target="tpu_custom_call" | custom-call | tf_op jit(solution)/shard_map/pallas_call | solution.py:383
  27.4 2.3 %shard_map.112 = (bf16[1,2,64,8,128]{4,3,2,1,0:T(8,128)(2,1)}, f32[2,64,128]{2,1,0:T(8,128)}, f32[2,64,128]{2,1,0:T(8,128)}, f32[2,64,128]{2,1,0:T(8,128)}) custom-call(f32[1024,128]{1,0:T(8,128)} %get-tuple-element.10.acc_in, f32[24,16,128]{2,1,0:T(8,128)} %get-tuple-element.11.w_in, bf16[1,2,64,8,128]{4,3,2,1,0:T(8,128)(2,1)} %up.3, s32[1,2,8,128]{3,2,1,0:T(8,128)} %usage.3), custom_call_target="tpu_custom_call" | custom-call | tf_op jit(solution)/shard_map/pallas_call | solution.py:428

commit v3 on v2

--- a/solution.py
+++ b/solution.py
@@ -38,7 +38,8 @@
 def kernel(
     pairs, strips, rows, cols, chunk,
     nodes, up, usage, blockage, capacity, w_src, w_dst, w_out,
-    acc, w_sum,
+    gn, w_sum,
+    acc, gv,
     xd, s_up, s_dn, gb, w1, pw, vw,
     nv, uv, usv, bv, cv, wsv, wdv, wov, t_rows, q_rows, in_sems,
     prev_x, next_x, prev_g, below, above, gps, wacc, wpart, wrecv, wres,
@@ -59,18 +60,6 @@
 
     barrier = pltpu.get_barrier_semaphore()
 
-    @pl.loop(1, devices)
-    def _(k):
-        pl.semaphore_signal(barrier, inc=1, device_id=place(k)[1], device_id_type=MESH)
-
-    stage(
-        pairs, strips,
-        nodes, up, usage, blockage, capacity, w_src, w_dst, w_out,
-        xd, s_up, s_dn, gb, w1, pw, vw,
-        nv, uv, usv, bv, cv, wsv, wdv, wov, t_rows, q_rows, in_sems,
-    )
-    pl.semaphore_wait(barrier, devices - 1)
-
     jr = lax.rem(p, 2)
     jc = 1 - jr
 
@@ -84,26 +73,44 @@
     def wait_bytes(ref, sem):
         pltpu.make_async_copy(ref, ref, sem).wait()
 
+    def greet():
+        @pl.loop(1, devices)
+        def _(k):
+            pl.semaphore_signal(barrier, inc=1, device_id=place(k)[1], device_id_type=MESH)
+
+    def ready():
+        pl.semaphore_wait(barrier, devices - 1)
+
+    def cross(j):
+        @pl.when((j == 1) & (p < pairs - 1))
+        def _():
+            @pl.loop(0, strips)
+            def _(k):
+                t = lax.rem(s + k, strips)
+                send(s_up.at[t], below.at[s], cross_send.at[0], cross_recv.at[0], (p + 1, t))
+
+        @pl.when((j == 0) & (p > 0))
+        def _():
+            @pl.loop(0, strips)
+            def _(k):
+                t = lax.rem(s + k, strips)
+                send(s_dn.at[t], above.at[s], cross_send.at[1], cross_recv.at[1], (p - 1, t))
+
+    stage_cells(
+        pairs, strips, greet, ready, cross,
+        nodes, up, usage, blockage, capacity, w_src, w_dst, w_out,
+        xd, s_up, s_dn,
+        nv, uv, usv, bv, cv, wsv, wdv, wov, t_rows, q_rows, in_sems,
+    )
     after = (p, lax.rem(s + 1, strips))
     before = (p, lax.rem(s + strips - 1, strips))
     last = pl.ds(cells - cols, cols)
-    halos = (
+    halos = [
         send(xd.at[jr, pl.ds(0, cols)], next_x, halo_send.at[0], halo_recv.at[0], before),
         send(xd.at[jr, last], prev_x, halo_send.at[1], halo_recv.at[1], after),
-        send(gb.at[jr, last], prev_g, halo_send.at[2], halo_recv.at[2], after),
-    )
-
-    @pl.loop(0, strips)
-    def _(k):
-        t = lax.rem(s + k, strips)
-
-        @pl.when(p < pairs - 1)
-        def _():
-            send(s_up.at[t], below.at[s], cross_send.at[0], cross_recv.at[0], (p + 1, t))
-
-        @pl.when(p > 0)
-        def _():
-            send(s_dn.at[t], above.at[s], cross_send.at[1], cross_recv.at[1], (p - 1, t))
+    ]
+    stage_rest(gb, w1, pw, vw, bv, cv, wsv, wdv, wov)
+    halos.append(send(gb.at[jr, last], prev_g, halo_send.at[2], halo_recv.at[2], after))
 
     starts = range(0, cells, step)
     for at in starts:
@@ -152,13 +159,14 @@
         part = jnp.concatenate((sd, o), 0).astype(BF16)
         wpart[pl.ds(kind * half, half)] = part.reshape(half, TILE, part.shape[1])
 
-        @pl.loop(1, devices)
-        def _(k):
-            target, to = place(k)
-
-            @pl.when((target >= kind * half) & (target < (kind + 1) * half))
-            def _():
-                send(wpart.at[target], wrecv.at[devices - 1 - k], red_send.at[0], red_recv.at[0], to)
+        for i in range(half):
+            target = kind * half + lax.rem(flat + i, half)
+
+            @pl.when(target != flat)
+            def _(target=target):
+                to = (lax.div(target, strips), lax.rem(target, strips))
+                slot = lax.rem(flat - target + devices, devices) - 1
+                send(wpart.at[target], wrecv.at[slot], red_send.at[0], red_recv.at[0], to)
 
     reduce_out(0)
 
@@ -200,6 +208,21 @@
 
     reduce_out(1)
 
+    half = feat * rows
+    for b in range(cols // LANES):
+        for r in range(rows):
+            tile = acc[pl.ds(r * cols + b * LANES, LANES)].T
+            t_rows[b, pl.ds(r, 2 * feat, stride=rows), :] = tile
+    for j in range(2):
+        damp = lax.rsqrt(1.0 + usv[0, j].astype(F32))
+        for b in range(cols // LANES):
+            cut = pl.ds(b * LANES, LANES)
+            ns = t_rows[b, pl.ds(j * half, half)].reshape(feat, rows, LANES)
+            scaled = damp[None, :, b * LANES : (b + 1) * LANES] * ns
+            gv[0, j, :, :, cut] = (uv[0, j, :, :, cut].astype(F32) + scaled).astype(BF16)
+    out_copy = pltpu.make_async_copy(gv, gn, in_sems.at[0])
+    out_copy.start()
+
     @pl.when(flat < owners)
     def _():
         wait_bytes(wrecv, red_recv.at[0])
@@ -229,41 +252,53 @@
         wait_bytes(s_dn, cross_send.at[1])
 
     w_sum[...] = wres[...].astype(F32)
+    out_copy.wait()
 
 
 LANES = 128
 
 
-def fetch(pairs_of_refs, sems):
+def fetch(pairs_of_refs, sems, meanwhile=None):
     copies = [pltpu.make_async_copy(a, b, sems.at[i]) for i, (a, b) in enumerate(pairs_of_refs)]
     for copy in copies:
         copy.start()
+    if meanwhile is not None:
+        meanwhile()
     for copy in copies:
         copy.wait()
 
 
-def stage(
-    pairs, strips,
+def stage_cells(
+    pairs, strips, greet, ready, cross,
     nodes, up, usage, blockage, capacity, w_src, w_dst, w_out,
-    xd, s_up, s_dn, gb, w1, pw, vw,
+    xd, s_up, s_dn,
     nv, uv, usv, bv, cv, wsv, wdv, wov, t, q, sems,
 ):
     p = lax.axis_index("lyr")
-    s = lax.axis_index("strip")
     fetch(
         (
             (nodes, nv), (up, uv), (usage, usv), (blockage, bv), (capacity, cv),
             (w_src, wsv), (w_dst, wdv), (w_out, wov),
         ),
         sems,
+        greet,
     )
     _, layers, feat, rows, cols = nv.shape
     lanes = 2 * feat
     half = feat * rows
     blocks = cols // LANES
-    damp = lax.rsqrt(1.0 + usv[0].astype(F32))
-    for j in range(layers):
-        x = (nv[0, j].astype(F32) * damp[j][None]).astype(BF16).astype(F32)
+    gates = (1 - bv[0, 1, 1]).astype(F32) * cv[0, 1, 1].astype(F32) * 0.25
+
+    def spread(j, out):
+        for r in range(rows):
+            q[pl.ds(r, cols, stride=rows), :] = xd[j, pl.ds(r * cols, cols)].astype(F32)
+        out[:, pl.ds(0, rows * rows), :] = q[...].astype(BF16).reshape(strips, rows * rows, lanes)
+
+    leading = 1 - lax.rem(p, 2)
+    for turn in range(layers):
+        j = leading if turn == 0 else 1 - leading
+        damp = lax.rsqrt(1.0 + usv[0, j].astype(F32))
+        x = (nv[0, j].astype(F32) * damp[None]).astype(BF16).astype(F32)
         d = uv[0, j].astype(F32)
         for b in range(blocks):
             cut = slice(b * LANES, (b + 1) * LANES)
@@ -274,27 +309,34 @@
                 m = t[b, pl.ds(r, lanes, stride=rows), :]
                 xd[j, pl.ds(r * cols + b * LANES, LANES)] = m.T.astype(BF16)
 
-    def spread(j, out):
-        for r in range(rows):
-            q[pl.ds(r, cols, stride=rows), :] = xd[j, pl.ds(r * cols, cols)].astype(F32)
-        out[:, pl.ds(0, rows * rows), :] = q[...].astype(BF16).reshape(strips, rows * rows, lanes)
-
-    @pl.when(p > 0)
-    def _():
-        spread(0, s_dn)
-
+        @pl.when((j == 0) & (p > 0))
+        def _():
+            spread(0, s_dn)
+
+        @pl.when((j == 1) & (p < pairs - 1))
+        def _():
+            spread(1, s_up)
+            per = LANES // rows
+            for b in range(blocks):
+                g = gates[:, b * LANES : (b + 1) * LANES]
+                g = jnp.concatenate((g, jnp.zeros((LANES - rows, LANES), F32)), 0).T
+                g = g.reshape(per, rows, LANES)
+                g = jnp.concatenate((g, jnp.zeros((per, TILE - rows, LANES), F32)), 1)
+                s_up[pl.ds(b * per, per), pl.ds(rows * rows, TILE), :] = g.astype(BF16)
+
+        if turn == 0:
+            ready()
+        cross(j)
+
+
+def stage_rest(gb, w1, pw, vw, bv, cv, wsv, wdv, wov):
+    p = lax.axis_index("lyr")
+    s = lax.axis_index("strip")
+    rows, cols = bv.shape[3:]
+    feat = wsv.shape[1]
+    lanes = 2 * feat
+    blocks = cols // LANES
     gates = (1 - bv[0]).astype(F32) * cv[0].astype(F32) * 0.25
-
-    @pl.when(p < pairs - 1)
-    def _():
-        spread(1, s_up)
-        per = LANES // rows
-        for b in range(blocks):
-            g = gates[1, 1][:, b * LANES : (b + 1) * LANES]
-            g = jnp.concatenate((g, jnp.zeros((LANES - rows, LANES), F32)), 0).T.reshape(per, rows, LANES)
-            g = jnp.concatenate((g, jnp.zeros((per, TILE - rows, LANES), F32)), 1)
-            s_up[pl.ds(b * per, per), pl.ds(rows * rows, TILE), :] = g.astype(BF16)
-
     row_ids = s * rows + lax.broadcasted_iota(jnp.int32, (rows, cols), 0)
     in_rows = (row_ids < cols - 1).astype(F32)
     in_cols = (lax.broadcasted_iota(jnp.int32, (rows, cols), 1) < cols - 1).astype(F32)
@@ -335,22 +377,11 @@
     vw[2] = jnp.concatenate((dst[1], none), 1)
 
 
-def finish(scale, acc_in, w_in, up, usage, gn, gs, gd, go, acc, w_sum, uv, usv, t, sems):
-    fetch(((acc_in, acc), (w_in, w_sum), (up, uv), (usage, usv)), sems)
-    _, layers, feat, rows, cols = uv.shape
+def finish(scale, gn_in, w_sum, gn, gs, gd, go, sem):
+    copy = pltpu.make_async_copy(gn_in, gn, sem)
+    copy.start()
+    feat = gs.shape[1]
     lanes = 2 * feat
-    half = feat * rows
-    blocks = cols // LANES
-    for b in range(blocks):
-        for r in range(rows):
-            t[b, pl.ds(r, lanes, stride=rows), :] = acc[pl.ds(r * cols + b * LANES, LANES)].T
-    damp = lax.rsqrt(1.0 + usv[0].astype(F32))
-    for j in range(layers):
-        for b in range(blocks):
-            cut = pl.ds(b * LANES, LANES)
-            ns = t[b, pl.ds(j * half, half)].reshape(feat, rows, LANES)
-            scaled = damp[j][None, :, b * LANES : (b + 1) * LANES] * ns
-            gn[0, j, :, :, cut] = (uv[0, j, :, :, cut].astype(F32) + scaled).astype(BF16)
     hidden = gs.shape[2]
     w = w_sum[...].reshape(2, 3 * hidden // 2, lanes) * scale
     for k in range(2):
@@ -359,6 +390,7 @@
         gd[k] = sd[feat:]
         o = w[k, hidden:]
         go[k] = jnp.concatenate((o[:, :feat], o[:, feat:]), 0).T
+    copy.wait()
 
 
 def on_device(nodes, upstream, usage, blockage, capacity, w_src, w_dst, w_out):
@@ -380,15 +412,17 @@
     def shape(dims, kind=BF16):
         return jax.ShapeDtypeStruct(dims, kind)
 
-    acc, w_sum = pl.pallas_call(
+    gn, w_sum = pl.pallas_call(
         functools.partial(kernel, pairs, strips, rows, cols, chunk),
         out_shape=(
-            jax.ShapeDtypeStruct((cells, lanes), F32),
+            shape(nodes.shape),
             jax.ShapeDtypeStruct((owners, TILE, lanes), F32),
         ),
         in_specs=[hbm] * 8,
-        out_specs=(vmem, vmem),
+        out_specs=(hbm, vmem),
         scratch_shapes=[
+            pltpu.VMEM((cells, lanes), F32),
+            pltpu.VMEM(nodes.shape, BF16),
             pltpu.VMEM((layers, cells, lanes), BF16),
             pltpu.VMEM((strips, rows * rows + TILE, lanes), BF16),
             pltpu.VMEM((strips, rows * rows, lanes), BF16),
@@ -433,18 +467,11 @@
             shape((2, feat, hidden), F32),
             shape(w_out.shape, F32),
         ),
-        in_specs=[hbm] * 4,
-        out_specs=(vmem,) * 4,
-        scratch_shapes=[
-            pltpu.VMEM(acc.shape, acc.dtype),
-            pltpu.VMEM(w_sum.shape, w_sum.dtype),
-            pltpu.VMEM(upstream.shape, upstream.dtype),
-            pltpu.VMEM(usage.shape, usage.dtype),
-            pltpu.VMEM((cols // LANES, lanes * rows, LANES), F32),
-            pltpu.SemaphoreType.DMA((4,)),
-        ],
+        in_specs=[hbm, vmem],
+        out_specs=(hbm, vmem, vmem, vmem),
+        scratch_shapes=[pltpu.SemaphoreType.DMA],
         compiler_params=params,
-    )(acc, w_sum, upstream, usage)
+    )(gn, w_sum)
     return gn, jnp.swapaxes(gs, 1, 2), jnp.swapaxes(gd, 1, 2), go
 
 

time: 29.8 us -> 39.4 us (1.32)
  Pallas kernels: 29 us -> 38.6 us
    pallas_call x1, Pallas kernels: 2.25 us -> 10.6 us  [on_device(): pl.pallas_call(functools.partial(finish, scale), out_shape=(shape(nodes.s...]
    pallas_call x1, Pallas kernels: 26.8 us -> 27.9 us  [on_device(): pl.pallas_call(functools.partial(kernel, pairs, strips, rows, cols, chunk...]
where the time goes in v3:
time: 39.4 us; the launch traced here: 39.2 us
  Pallas kernels  38.6 us (98%)
  between operations  0.64 us (2%)
    pallas_call x1, Pallas kernels, on_device(): pl.pallas_call(functools.partial(kernel, pairs, strips, rows, cols, chunk...  27.9 us
    pallas_call x1, Pallas kernels, on_device(): pl.pallas_call(functools.partial(finish, scale), out_shape=(shape(nodes.s...  10.6 us

profile of v3, /device:TPU:0, one launch (start us, length us, event | category | flops | bytes accessed | tf_op | source)
XLA Modules:
  0.0 39.2 jit_solution(12508431174052416789)
XLA Ops:
  0.6 27.9 %shard_map.111 = (bf16[1,2,64,8,128]{4,3,2,1,0:T(8,128)(2,1)}, f32[24,16,128]{2,1,0:T(8,128)}) custom-call(bf16[1,2,64,8,128]{4,3,2,1,0:T(8,128)(2,1)} %nodes.1, bf16[1,2,64,8,128]{4,3,2,1,0:T(8,128)(2,1)} %up.1, s32[1,2,8,128]{3,2,1,0:T(8,128)} %usage.1, s32[1,2,2,8,128]{4,3,2,1,0:T(8,128)} %blockage.1, s32[1,2,2,8,128]{4,3,2,1,0:T(8,128)} %capacity.1, ...), custom_call_target="tpu_custom_call" | custom-call | tf_op jit(solution)/shard_map/pallas_call | solution.py:415
  28.6 10.6 %shard_map.112 = (bf16[1,2,64,8,128]{4,3,2,1,0:T(8,128)(2,1)}, f32[2,64,128]{2,1,0:T(8,128)}, f32[2,64,128]{2,1,0:T(8,128)}, f32[2,64,128]{2,1,0:T(8,128)}) custom-call(bf16[1,2,64,8,128]{4,3,2,1,0:T(8,128)(2,1)} %get-tuple-element.10.gn_in, f32[24,16,128]{2,1,0:T(8,128)} %get-tuple-element.11.w_sum), custom_call_target="tpu_custom_call" | custom-call | tf_op jit(solution)/shard_map/pallas_call | solution.py:462

commit v4 on v3

--- a/solution.py
+++ b/solution.py
@@ -38,8 +38,8 @@
 def kernel(
     pairs, strips, rows, cols, chunk,
     nodes, up, usage, blockage, capacity, w_src, w_dst, w_out,
-    gn, w_sum,
-    acc, gv,
+    acc_out, w_sum,
+    acc,
     xd, s_up, s_dn, gb, w1, pw, vw,
     nv, uv, usv, bv, cv, wsv, wdv, wov, t_rows, q_rows, in_sems,
     prev_x, next_x, prev_g, below, above, gps, wacc, wpart, wrecv, wres,
@@ -208,19 +208,7 @@
 
     reduce_out(1)
 
-    half = feat * rows
-    for b in range(cols // LANES):
-        for r in range(rows):
-            tile = acc[pl.ds(r * cols + b * LANES, LANES)].T
-            t_rows[b, pl.ds(r, 2 * feat, stride=rows), :] = tile
-    for j in range(2):
-        damp = lax.rsqrt(1.0 + usv[0, j].astype(F32))
-        for b in range(cols // LANES):
-            cut = pl.ds(b * LANES, LANES)
-            ns = t_rows[b, pl.ds(j * half, half)].reshape(feat, rows, LANES)
-            scaled = damp[None, :, b * LANES : (b + 1) * LANES] * ns
-            gv[0, j, :, :, cut] = (uv[0, j, :, :, cut].astype(F32) + scaled).astype(BF16)
-    out_copy = pltpu.make_async_copy(gv, gn, in_sems.at[0])
+    out_copy = pltpu.make_async_copy(acc, acc_out, in_sems.at[0])
     out_copy.start()
 
     @pl.when(flat < owners)
@@ -377,11 +365,22 @@
     vw[2] = jnp.concatenate((dst[1], none), 1)
 
 
-def finish(scale, gn_in, w_sum, gn, gs, gd, go, sem):
-    copy = pltpu.make_async_copy(gn_in, gn, sem)
-    copy.start()
-    feat = gs.shape[1]
+def finish(scale, acc_in, w_in, up, usage, gn, gs, gd, go, acc, w_sum, uv, usv, t, sems):
+    fetch(((acc_in, acc), (w_in, w_sum), (up, uv), (usage, usv)), sems)
+    _, layers, feat, rows, cols = uv.shape
     lanes = 2 * feat
+    half = feat * rows
+    blocks = cols // LANES
+    for b in range(blocks):
+        for r in range(rows):
+            t[b, pl.ds(r, lanes, stride=rows), :] = acc[pl.ds(r * cols + b * LANES, LANES)].T
+    damp = lax.rsqrt(1.0 + usv[0].astype(F32))
+    for j in range(layers):
+        for b in range(blocks):
+            cut = pl.ds(b * LANES, LANES)
+            ns = t[b, pl.ds(j * half, half)].reshape(feat, rows, LANES)
+            scaled = damp[j][None, :, b * LANES : (b + 1) * LANES] * ns
+            gn[0, j, :, :, cut] = (uv[0, j, :, :, cut].astype(F32) + scaled).astype(BF16)
     hidden = gs.shape[2]
     w = w_sum[...].reshape(2, 3 * hidden // 2, lanes) * scale
     for k in range(2):
@@ -390,7 +389,6 @@
         gd[k] = sd[feat:]
         o = w[k, hidden:]
         go[k] = jnp.concatenate((o[:, :feat], o[:, feat:]), 0).T
-    copy.wait()
 
 
 def on_device(nodes, upstream, usage, blockage, capacity, w_src, w_dst, w_out):
@@ -412,17 +410,16 @@
     def shape(dims, kind=BF16):
         return jax.ShapeDtypeStruct(dims, kind)
 
-    gn, w_sum = pl.pallas_call(
+    acc, w_sum = pl.pallas_call(
         functools.partial(kernel, pairs, strips, rows, cols, chunk),
         out_shape=(
-            shape(nodes.shape),
+            shape((cells, lanes), F32),
             jax.ShapeDtypeStruct((owners, TILE, lanes), F32),
         ),
         in_specs=[hbm] * 8,
         out_specs=(hbm, vmem),
         scratch_shapes=[
             pltpu.VMEM((cells, lanes), F32),
-            pltpu.VMEM(nodes.shape, BF16),
             pltpu.VMEM((layers, cells, lanes), BF16),
             pltpu.VMEM((strips, rows * rows + TILE, lanes), BF16),
             pltpu.VMEM((strips, rows * rows, lanes), BF16),
@@ -467,11 +464,18 @@
             shape((2, feat, hidden), F32),
             shape(w_out.shape, F32),
         ),
-        in_specs=[hbm, vmem],
-        out_specs=(hbm, vmem, vmem, vmem),
-        scratch_shapes=[pltpu.SemaphoreType.DMA],
+        in_specs=[hbm] * 4,
+        out_specs=(vmem,) * 4,
+        scratch_shapes=[
+            pltpu.VMEM(acc.shape, acc.dtype),
+            pltpu.VMEM(w_sum.shape, w_sum.dtype),
+            pltpu.VMEM(upstream.shape, upstream.dtype),
+            pltpu.VMEM(usage.shape, usage.dtype),
+            pltpu.VMEM((cols // LANES, lanes * rows, LANES), F32),
+            pltpu.SemaphoreType.DMA((4,)),
+        ],
         compiler_params=params,
-    )(gn, w_sum)
+    )(acc, w_sum, upstream, usage)
     return gn, jnp.swapaxes(gs, 1, 2), jnp.swapaxes(gd, 1, 2), go
 
 

time: 39.4 us -> 31 us (0.79)
  Pallas kernels: 38.6 us -> 30.2 us
    pallas_call x1, Pallas kernels: 10.6 us -> 2.25 us  [on_device(): pl.pallas_call(functools.partial(finish, scale), out_shape=(shape(nodes.s...]
where the time goes in v4:
time: 31 us; the launch traced here: 30.8 us
  Pallas kernels  30.2 us (97%)
  between operations  0.64 us (2%)
    pallas_call x1, Pallas kernels, on_device(): pl.pallas_call(functools.partial(kernel, pairs, strips, rows, cols, chunk...  27.9 us
    pallas_call x1, Pallas kernels, on_device(): pl.pallas_call(functools.partial(finish, scale), out_shape=(shape(nodes.s...  2.25 us

profile of v4, /device:TPU:0, one launch (start us, length us, event | category | flops | bytes accessed | tf_op | source)
XLA Modules:
  0.0 30.8 jit_solution(368828074026726619)
XLA Ops:
  0.6 27.9 %shard_map.111 = (f32[1024,128]{1,0:T(8,128)}, f32[24,16,128]{2,1,0:T(8,128)}) custom-call(bf16[1,2,64,8,128]{4,3,2,1,0:T(8,128)(2,1)} %nodes.1, bf16[1,2,64,8,128]{4,3,2,1,0:T(8,128)(2,1)} %up.3, s32[1,2,8,128]{3,2,1,0:T(8,128)} %usage.3, s32[1,2,2,8,128]{4,3,2,1,0:T(8,128)} %blockage.1, s32[1,2,2,8,128]{4,3,2,1,0:T(8,128)} %capacity.1, ...), custom_call_target="tpu_custom_call" | custom-call | tf_op jit(solution)/shard_map/pallas_call | solution.py:413
  28.6 2.3 %shard_map.112 = (bf16[1,2,64,8,128]{4,3,2,1,0:T(8,128)(2,1)}, f32[2,64,128]{2,1,0:T(8,128)}, f32[2,64,128]{2,1,0:T(8,128)}, f32[2,64,128]{2,1,0:T(8,128)}) custom-call(f32[1024,128]{1,0:T(8,128)} %get-tuple-element.10.acc_in, f32[24,16,128]{2,1,0:T(8,128)} %get-tuple-element.11.w_in, bf16[1,2,64,8,128]{4,3,2,1,0:T(8,128)(2,1)} %up.3, s32[1,2,8,128]{3,2,1,0:T(8,128)} %usage.3), custom_call_target="tpu_custom_call" | custom-call | tf_op jit(solution)/shard_map/pallas_call | solution.py:459

commit v5 on v2

--- a/solution.py
+++ b/solution.py
@@ -59,12 +59,13 @@
 
     barrier = pltpu.get_barrier_semaphore()
 
-    @pl.loop(1, devices)
-    def _(k):
-        pl.semaphore_signal(barrier, inc=1, device_id=place(k)[1], device_id_type=MESH)
+    def greet():
+        @pl.loop(1, devices)
+        def _(k):
+            pl.semaphore_signal(barrier, inc=1, device_id=place(k)[1], device_id_type=MESH)
 
     stage(
-        pairs, strips,
+        pairs, strips, greet,
         nodes, up, usage, blockage, capacity, w_src, w_dst, w_out,
         xd, s_up, s_dn, gb, w1, pw, vw,
         nv, uv, usv, bv, cv, wsv, wdv, wov, t_rows, q_rows, in_sems,
@@ -234,16 +235,18 @@
 LANES = 128
 
 
-def fetch(pairs_of_refs, sems):
+def fetch(pairs_of_refs, sems, meanwhile=None):
     copies = [pltpu.make_async_copy(a, b, sems.at[i]) for i, (a, b) in enumerate(pairs_of_refs)]
     for copy in copies:
         copy.start()
+    if meanwhile is not None:
+        meanwhile()
     for copy in copies:
         copy.wait()
 
 
 def stage(
-    pairs, strips,
+    pairs, strips, greet,
     nodes, up, usage, blockage, capacity, w_src, w_dst, w_out,
     xd, s_up, s_dn, gb, w1, pw, vw,
     nv, uv, usv, bv, cv, wsv, wdv, wov, t, q, sems,
@@ -256,6 +259,7 @@
             (w_src, wsv), (w_dst, wdv), (w_out, wov),
         ),
         sems,
+        greet,
     )
     _, layers, feat, rows, cols = nv.shape
     lanes = 2 * feat

time: 29.8 us -> 29.7 us (level)
  no operation moved by 1% of the time
where the time goes in v5:
time: 29.7 us; the launch traced here: 29.6 us
  Pallas kernels  28.9 us (97%)
  between operations  0.64 us (2%)
    pallas_call x1, Pallas kernels, on_device(): pl.pallas_call(functools.partial(kernel, pairs, strips, rows, cols, chunk...  26.7 us
    pallas_call x1, Pallas kernels, on_device(): pl.pallas_call(functools.partial(finish, scale), out_shape=(shape(nodes.s...  2.25 us

profile of v5, /device:TPU:0, one launch (start us, length us, event | category | flops | bytes accessed | tf_op | source)
XLA Modules:
  0.0 29.6 jit_solution(17330163713771505788)
XLA Ops:
  0.6 26.7 %shard_map.111 = (f32[1024,128]{1,0:T(8,128)}, f32[24,16,128]{2,1,0:T(8,128)}) custom-call(bf16[1,2,64,8,128]{4,3,2,1,0:T(8,128)(2,1)} %nodes.1, bf16[1,2,64,8,128]{4,3,2,1,0:T(8,128)(2,1)} %up.3, s32[1,2,8,128]{3,2,1,0:T(8,128)} %usage.3, s32[1,2,2,8,128]{4,3,2,1,0:T(8,128)} %blockage.1, s32[1,2,2,8,128]{4,3,2,1,0:T(8,128)} %capacity.1, ...), custom_call_target="tpu_custom_call" | custom-call | tf_op jit(solution)/shard_map/pallas_call | solution.py:387
  27.3 2.3 %shard_map.112 = (bf16[1,2,64,8,128]{4,3,2,1,0:T(8,128)(2,1)}, f32[2,64,128]{2,1,0:T(8,128)}, f32[2,64,128]{2,1,0:T(8,128)}, f32[2,64,128]{2,1,0:T(8,128)}) custom-call(f32[1024,128]{1,0:T(8,128)} %get-tuple-element.10.acc_in, f32[24,16,128]{2,1,0:T(8,128)} %get-tuple-element.11.w_in, bf16[1,2,64,8,128]{4,3,2,1,0:T(8,128)(2,1)} %up.3, s32[1,2,8,128]{3,2,1,0:T(8,128)} %usage.3), custom_call_target="tpu_custom_call" | custom-call | tf_op jit(solution)/shard_map/pallas_call | solution.py:432
